TPU v7x, 32 devices: a whole 2x2x4 slice. The times are simulated.
32 devices in a mesh: offset: 1, slab: 32 (over z, y, x, core).
Axes of the slice: x: 2, y: 2, z: 4, core: 2. Of those that a mesh axis runs over, the one named last changes fastest.
Arguments:
- traces: bfloat16 [1, 4096, 256], P('offset', 'slab'), may hold values from -6 to 6
- centre_ids: int32 [1, 4096, 1], P('offset', 'slab'), may hold values from 0 to 31; in each aligned block of 128 rows (0 to 127, 128 to 255, ..., all dimensions but the last counted through in order) at most 6 rows name the same one
- midpoint_bins: int32 [1, 4096], P('offset', 'slab'), may hold values from 0 to 15
- ray_times: float32 [1, 32, 7, 16, 256], P('offset', 'slab'), may hold values from 16 to 240
- ray_amps: float32 [1, 32, 7, 16, 256], P('offset', 'slab'), may hold values from 0.2 to 2
- beam_lateral: float32 [1, 32, 7, 16], P('offset'), may hold values from 0 to 128
- footprint: int32 [32, 7, 2], replicated, may hold values from 0 to 128, as said below
Outputs:
- image: float32 [256, 4096], P('offset', 'slab')
Inputs may be any that keep to these rules, and one draw needn't show every extreme that they name: `centre_ids`: within the rows of one device no centre is named by more than 6 rows. footprint[c, w, 0] is below 64 and footprint[c, w, 1] above it; at w = 3, a centre's own slab, they are 0 and 128.
All inputs are finite; a program needn't handle non-finite values.
Results may differ from a plain program's by a relative error of at most 0.0049.
Values may be sent and summed in bfloat16 or wider, within the bound.
A program may use at most 64 MiB of HBM per device.

v0:
```python
import math

import jax
import jax.numpy as jnp
from jax import lax
from jax.sharding import PartitionSpec as P

NT = 256
NF = 64
KLO = 8
P_SIZE = 16
BINS = 16
CAP = 6
WIN = 7
XW = 128


two_pi = 2.0 * math.pi
slow_step = 0.25
width_scale = 200.0


def shifted(shard, axis, by):
    count = lax.axis_size(axis)
    pairs = [(i, i + by) for i in range(count) if 0 <= i + by < count]
    return lax.ppermute(shard, axis, pairs)


def dft_table():
    sample = jnp.arange(NT, dtype=jnp.int32)[:, None]
    bin_index = jnp.arange(NF, dtype=jnp.int32)[None, :] + KLO
    turns = (sample * bin_index % NT).astype(jnp.float32) * (two_pi / NT)
    return jnp.concatenate([jnp.cos(turns), -jnp.sin(turns)], axis=1)


def omegas():
    return (jnp.arange(NF, dtype=jnp.int32) + KLO).astype(jnp.float32) * (two_pi / NT)


def slowness():
    return (
        jnp.arange(P_SIZE, dtype=jnp.int32).astype(jnp.float32) - (P_SIZE - 1) / 2.0
    ) * slow_step


def beam_blocks(beams, times_in, amps_in, lateral, first_col, end_col):
    freq = omegas()
    phase = freq[None, :, None] * times_in[:, None, :]
    depth = times_in.shape[1]
    u_block = jnp.stack(
        [amps_in[:, None, :] * jnp.cos(phase), -amps_in[:, None, :] * jnp.sin(phase)]
    )
    u_block = u_block.reshape(2 * P_SIZE * NF, depth).astype(jnp.bfloat16)
    col_index = jnp.arange(XW, dtype=jnp.int32)
    inside = ((col_index >= first_col) & (col_index < end_col)).astype(jnp.float32)
    columns = col_index.astype(jnp.float32)
    gauss = jnp.exp(
        -((columns[None, None, :] - lateral[:, None, None]) ** 2)
        * freq[None, :, None]
        / width_scale
    )
    gauss = gauss * inside[None, None, :] / math.sqrt(P_SIZE * NF)
    beam_re = beams[:, :NF].astype(jnp.float32)[:, :, None]
    beam_im = beams[:, NF:].astype(jnp.float32)[:, :, None]
    v_block = (
        jnp.stack([beam_re * gauss, beam_im * gauss])
        .reshape(2 * P_SIZE * NF, XW)
        .astype(jnp.bfloat16)
    )
    return lax.dot_general(
        u_block, v_block, (((0,), (0,)), ((), ())), preferred_element_type=jnp.float32
    )


def shards(traces, centre_ids, midpoint_bins, ray_times, ray_amps, beam_lateral, footprint):
    my_slab = lax.axis_index("slab")
    slab_count = lax.axis_size("slab")
    half_win = (WIN - 1) // 2
    centre_of = centre_ids[0, :, 0]
    one_hot = (centre_of[:, None] == jnp.arange(slab_count, dtype=jnp.int32)[None, :]).astype(
        jnp.int32
    )
    slot_rank = jnp.sum((jnp.cumsum(one_hot, axis=0) - 1) * one_hot, axis=1)
    target_row = centre_of * CAP + slot_rank
    samples = jnp.zeros((slab_count * CAP, NT), jnp.bfloat16).at[target_row].set(traces[0])
    places = (midpoint_bins[0].astype(jnp.float32) - (BINS - 1) / 2.0).astype(jnp.bfloat16)
    place_slots = jnp.zeros((slab_count * CAP,), jnp.bfloat16).at[target_row].set(places)
    arrived, arrived_place = (
        lax.all_to_all(
            samples.reshape(slab_count, CAP, NT), "slab", split_axis=0, concat_axis=0, tiled=True
        ),
        lax.all_to_all(
            place_slots.reshape(slab_count, CAP), "slab", split_axis=0, concat_axis=0, tiled=True
        ),
    )
    spectrum = jnp.dot(
        arrived.reshape(slab_count * CAP, NT).astype(jnp.float32),
        dft_table(),
        precision=lax.Precision.HIGHEST,
    )
    position = arrived_place.reshape(slab_count * CAP).astype(jnp.float32)
    phase = omegas()[None, None, :] * slowness()[None, :, None] * position[:, None, None]
    cosine = jnp.cos(phase)
    sine_part = jnp.sin(phase)
    spec_re = spectrum[:, None, :NF]
    spec_im = spectrum[:, None, NF:]
    beam_re = jnp.sum(spec_re * cosine + spec_im * sine_part, axis=0)
    beam_im = jnp.sum(spec_im * cosine - spec_re * sine_part, axis=0)
    scale = 1.0 / math.sqrt(NT * traces.shape[1])
    beams = (jnp.concatenate([beam_re, beam_im], axis=1) * scale).astype(jnp.bfloat16)
    depth = ray_times.shape[4]
    partial_image = jnp.zeros((depth, XW), jnp.float32)
    lateral_own = lax.dynamic_index_in_dim(beam_lateral[0], my_slab, 0, keepdims=False)
    foot_own = lax.dynamic_index_in_dim(footprint, my_slab, 0, keepdims=False)
    for window in range(WIN):
        step_by = window - half_win
        contrib = beam_blocks(
            beams,
            ray_times[0, 0, window],
            ray_amps[0, 0, window],
            lateral_own[window],
            foot_own[window, 0],
            foot_own[window, 1],
        )
        if step_by == 0:
            partial_image = partial_image + contrib
        else:
            partial_image = partial_image + shifted(contrib, "slab", step_by)
    return lax.psum_scatter(partial_image, "offset", scatter_dimension=0, tiled=True)


def solution(mesh):
    return jax.shard_map(
        shards,
        mesh=mesh,
        in_specs=(
            P("offset", "slab", None),
            P("offset", "slab", None),
            P("offset", "slab"),
            P("offset", "slab", None, None, None),
            P("offset", "slab", None, None, None),
            P("offset", None, None, None),
            P(),
        ),
        out_specs=P("offset", "slab"),
        check_vma=False,
    )
```

profile of v0, /device:TPU:9, one launch (start us, length us, event | category | flops | bytes accessed | tf_op | source)
XLA Modules:
  0.0 99.6 jit_solution(9286934645187517765)
XLA Ops:
  0.0 0.7 convert_bitcast_fusion
  0.7 0.7 copy-done.14
  1.4 0.1 fusion.91
  1.4 0.2 reduce_window_sum.11
  1.6 0.2 select_reduce_fusion
  1.8 1.3 %scatter_custom_fusion.1 = bf16[192]{0:T(256)(128)(2,1)S(1)} fusion(s32[128]{0:T(128)S(1)} %fusion.94, bf16[128]{0:T(256)(128)(2,1)S(1)} %convert_bitcast_fusion, bf16[]{:T(256)} %constant.69.clone.1), kind=kCustom, calls=%fused_computation.196 | custom fusion | bytes 386 | tf_op jit(solution)/shard_map/scatter | solution.py:87
  3.2 0.7 all_to_all.12
  3.9 6.4 %all-to-all-start.1 = ((bf16[32,1,6]{2,1,0:T(2,128)(2,1)}), bf16[32,1,6]{2,1,0:T(2,128)(2,1)S(1)}, u32[]{:S(2)}, u32[]{:S(2)}) async-start(bf16[32,1,6]{2,1,0:T(2,128)(2,1)} %all_to_all.12), calls=%async_computation.1 | async-start | bytes 32768 | tf_op jit(solution)/shard_map/all_to_all | solution.py:92
  10.3 0.7 copy-done.13
  11.1 0.1 copy.12
  11.2 0.7 fusion.117
  11.9 0.9 copy-done.11
  12.8 0.5 fusion.90
  13.4 4.2 %fusion.9 = (bf16[1,16,64,256]{3,2,1,0:T(8,128)(2,1)S(1)}, bf16[1,16,64,256]{3,2,1,0:T(8,128)(2,1)S(1)}) fusion(f32[16,256]{1,0:T(8,128)S(1)} %get-tuple-element.25, f32[64]{0:T(128)S(1)} %convert_multiply_fusion.2, f32[16,256]{1,0:T(8,128)S(1)} %get-tuple-element.144, f32[16,256]{1,0:T(8,128)S(1)} %get-tuple-element.34), kind=kLoop, calls=%fused_computation.34 | loop fusion | flops 1310720 | bytes 1097984 | tf_op jit(solution)/shard_map/convert.27
  17.6 2.5 %and_convert_fusion.2 = (f32[128]{0:T(128)S(1)}, f32[128]{0:T(128)S(1)}) fusion(s32[]{:T(128)} %bitcast.34, s32[]{:T(128)} %bitcast.33, s32[]{:T(128)} %bitcast.28, s32[]{:T(128)} %bitcast.27), kind=kLoop, calls=%fused_computation.184 | loop fusion | flops 1024 | bytes 1040 | tf_op jit(solution)/shard_map/convert_element_type | solution.py:55
  20.1 2.4 %and_convert_fusion = (f32[128]{0:T(128)S(1)}, f32[128]{0:T(128)S(1)}) fusion(s32[]{:T(128)} %bitcast.46, s32[]{:T(128)} %bitcast.45, s32[]{:T(128)} %bitcast.40, s32[]{:T(128)} %bitcast.39), kind=kLoop, calls=%fused_computation.182 | loop fusion | flops 1024 | bytes 1040 | tf_op jit(solution)/shard_map/convert_element_type | solution.py:55
  22.5 0.3 dynamic-slice_reduce_fusion.3
  22.8 0.1 multiply_negate_fusion.3
  22.9 24.6 %fusion.21 = (bf16[1,16,64,256]{3,2,1,0:T(8,128)(2,1)S(1)}, bf16[1,16,64,256]{3,2,1,0:T(8,128)(2,1)S(1)}, bf16[1,16,64,256]{3,2,1,0:T(8,128)(2,1)}, bf16[1,16,64...) fusion(f32[16,256]{1,0:T(8,128)S(1)} %get-tuple-element.21, ...), kind=kLoop, calls=%fused_computation.46 | loop fusion | flops 7864320 | bytes 6586624 | tf_op jit(solution)/shard_map/convert.15
  47.6 2.5 %and_convert_fusion.4 = (f32[128]{0:T(128)S(1)}, f32[128]{0:T(128)S(1)}) fusion(s32[]{:T(128)} %bitcast.22, s32[]{:T(128)} %bitcast.21, s32[]{:T(128)} %bitcast.16, s32[]{:T(128)} %bitcast.15), kind=kLoop, calls=%fused_computation.186 | loop fusion | flops 1024 | bytes 1040 | tf_op jit(solution)/shard_map/convert_element_type | solution.py:55
  50.1 1.1 %scatter_custom_fusion = bf16[192,256]{1,0:T(8,128)(2,1)S(1)} fusion(s32[128]{0:T(128)S(1)} %fusion.94, bf16[1,128,256]{2,1,0:T(8,128)(2,1)S(1)} %copy-done, bf16[]{:T(256)} %constant.69.clone.1), kind=kCustom, calls=%fused_computation.139 | custom fusion | bytes 163842 | tf_op jit(solution)/shard_map/scatter | solution.py:85
  51.2 0.7 reshape.749
  51.9 5.8 %all-to-all-start = ((bf16[32,6,256]{2,1,0:T(8,128)(2,1)}), bf16[32,6,256]{2,1,0:T(8,128)(2,1)S(1)}, u32[]{:S(2)}, u32[]{:S(2)}) async-start(bf16[32,6,256]{2,1,0:T(8,128)(2,1)} %reshape.749), calls=%async_computation | async-start | bytes 262144 | tf_op jit(solution)/shard_map/all_to_all | solution.py:89
  57.7 1.2 %and_convert_fusion.6 = f32[128]{0:T(128)S(1)} fusion(s32[]{:T(128)} %bitcast.4, s32[]{:T(128)} %bitcast.3), kind=kLoop, calls=%fused_computation.188 | loop fusion | flops 512 | bytes 520 | tf_op jit(solution)/shard_map/convert_element_type | solution.py:55
  59.0 0.1 reshape.751
  59.1 4.7 %all-to-all-done = bf16[32,6,256]{2,1,0:T(8,128)(2,1)S(1)} async-done(((bf16[32,6,256]{2,1,0:T(8,128)(2,1)}), bf16[32,6,256]{2,1,0:T(8,128)(2,1)S(1)}, u32[]{:S(2)}, u32[]{:S(2)}) %all-to-all-start) | async-done | bytes 98336 | tf_op jit(solution)/shard_map/all_to_all | solution.py:89
  63.9 0.3 fusion.81
  64.2 0.1 fusion.116
  64.3 0.1 copy.13
  64.4 0.1 copy.15
  64.5 4.7 %fusion.5 = (f32[16,64]{1,0:T(8,128)S(1)}, f32[16,64]{1,0:T(8,128)S(1)}) fusion(f32[192,64]{0,1:T(8,128)S(1)} %copy.15, f32[192]{0:T(256)S(1)} %reshape.751, f32[16,64]{1,0:T(8,128)S(1)} %broadcast_multiply_fusion, f32[192,64]{0,1:T(8,128)S(1)} %copy.13), kind=kLoop, calls=%fused_computation.30 | loop fusion | flops 1767424 | bytes 111360 | tf_op jit(solution)/shard_map/reduce_sum | solution.py:107
  69.2 0.1 fusion.93
  69.4 1.5 %multiply_convert_fusion.1 = (bf16[1,16,64,128]{3,2,1,0:T(8,128)(2,1)S(1)}, bf16[1,16,64,128]{3,2,1,0:T(8,128)(2,1)S(1)}, bf16[1,16,64,128]{3,2,1,0:T(8,128)(2,1...) fusion(f32[128]{0:T(128)S(1)} %get-tuple-element.149, ...), kind=kLoop, calls=%fused_computation.104 | loop fusion | flops 6422528 | bytes 3739392 | tf_op jit(solution)/shard_map/convert.1
  70.9 0.5 convolution_bitcast_fusion.6
  71.4 4.5 %collective-permute-start = (f32[256,128]{1,0:T(8,128)S(1)}, f32[256,128]{1,0:T(8,128)S(1)}, u32[]{:S(2)}, u32[]{:S(2)}) collective-permute-start(f32[256,128]{1,0:T(8,128)S(1)} %convolution_bitcast_fusion.6), channel_id=1, source_target_pairs={{3,0},{4,1},{5,2},{6,3},{7,4},{8,5},{9,6},{10,7},{11,8},{12,9},{13... | collective-permute-start | bytes 393224 | tf_op jit(solution)/shard_map/ppermute | solution.py:26
  76.0 0.5 convolution_bitcast_fusion.5
  76.5 2.9 %collective-permute-start.1 = (f32[256,128]{1,0:T(8,128)S(1)}, f32[256,128]{1,0:T(8,128)S(1)}, u32[]{:S(2)}, u32[]{:S(2)}) collective-permute-start(f32[256,128]{1,0:T(8,128)S(1)} %convolution_bitcast_fusion.5), channel_id=1, source_target_pairs={{2,0},{3,1},{4,2},{5,3},{6,4},{7,5},{8,6},{9,7},{10,8},{11,9},{12,... | collective-permute-start | bytes 393224 | tf_op jit(solution)/shard_map/ppermute | solution.py:26
  79.4 0.5 convolution_bitcast_fusion.4
  79.9 2.1 %collective-permute-start.2 = (f32[256,128]{1,0:T(8,128)S(1)}, f32[256,128]{1,0:T(8,128)S(1)}, u32[]{:S(2)}, u32[]{:S(2)}) collective-permute-start(f32[256,128]{1,0:T(8,128)S(1)} %convolution_bitcast_fusion.4), channel_id=1, source_target_pairs={{1,0},{2,1},{3,2},{4,3},{5,4},{6,5},{7,6},{8,7},{9,8},{10,9},{11,1... | collective-permute-start | bytes 393224 | tf_op jit(solution)/shard_map/ppermute | solution.py:26
  82.1 0.5 convolution_bitcast_fusion.2
  82.5 3.5 %collective-permute-start.3 = (f32[256,128]{1,0:T(8,128)S(1)}, f32[256,128]{1,0:T(8,128)S(1)}, u32[]{:S(2)}, u32[]{:S(2)}) collective-permute-start(f32[256,128]{1,0:T(8,128)S(1)} %convolution_bitcast_fusion.2), channel_id=1, source_target_pairs={{0,1},{1,2},{2,3},{3,4},{4,5},{5,6},{6,7},{7,8},{8,9},{9,10},{10,1... | collective-permute-start | bytes 393224 | tf_op jit(solution)/shard_map/ppermute | solution.py:26
  86.1 0.5 convolution_bitcast_fusion.1
  86.5 3.3 %collective-permute-start.4 = (f32[256,128]{1,0:T(8,128)S(1)}, f32[256,128]{1,0:T(8,128)S(1)}, u32[]{:S(2)}, u32[]{:S(2)}) collective-permute-start(f32[256,128]{1,0:T(8,128)S(1)} %convolution_bitcast_fusion.1), channel_id=1, source_target_pairs={{0,2},{1,3},{2,4},{3,5},{4,6},{5,7},{6,8},{7,9},{8,10},{9,11},{10,... | collective-permute-start | bytes 393224 | tf_op jit(solution)/shard_map/ppermute | solution.py:26
  89.9 0.5 convolution_bitcast_fusion
  90.4 1.9 %collective-permute-start.5 = (f32[256,128]{1,0:T(8,128)S(1)}, f32[256,128]{1,0:T(8,128)S(1)}, u32[]{:S(2)}, u32[]{:S(2)}) collective-permute-start(f32[256,128]{1,0:T(8,128)S(1)} %convolution_bitcast_fusion), channel_id=1, source_target_pairs={{0,3},{1,4},{2,5},{3,6},{4,7},{5,8},{6,9},{7,10},{8,11},{9,12},{10... | collective-permute-start | bytes 393224 | tf_op jit(solution)/shard_map/ppermute | solution.py:26
  92.3 3.5 %collective-permute-done.4 = f32[256,128]{1,0:T(8,128)S(1)} collective-permute-done((f32[256,128]{1,0:T(8,128)S(1)}, f32[256,128]{1,0:T(8,128)S(1)}, u32[]{:S(2)}, u32[]{:S(2)}) %collective-permute-start.4) | collective-permute-done | bytes 131104 | tf_op jit(solution)/shard_map/ppermute | solution.py:26
  95.8 2.6 %collective-permute-done.5 = f32[256,128]{1,0:T(8,128)S(1)} collective-permute-done((f32[256,128]{1,0:T(8,128)S(1)}, f32[256,128]{1,0:T(8,128)S(1)}, u32[]{:S(2)}, u32[]{:S(2)}) %collective-permute-start.5) | collective-permute-done | bytes 131104 | tf_op jit(solution)/shard_map/ppermute | solution.py:26
  98.4 1.1 %add_add_fusion = f32[256,128]{1,0:T(8,128)} fusion(f32[256,128]{1,0:T(8,128)S(1)} %collective-permute-done.5, f32[256,128]{1,0:T(8,128)S(1)} %collective-permute-done.4, f32[256,128]{1,0:T(8,128)S(1)} %collective-permute-done.3, f32[256,128]{1,0:T(8,128)S(1)} %collective-permute-done.2, f32[256,128]{1,0:T(8,128)S(1)} %collective-permute-done, ...), kind=kOutput, calls=%fused_computation.134 | convolution fusion | flops 135200768 | bytes 2490368 | tf_op jit(solution)/shard_map/dot_general | solution.py:70
  (44 shorter events, 0.4 us)
Async XLA Ops:
  0.0 50.1 %copy-start = (bf16[1,128,256]{2,1,0:T(8,128)(2,1)S(1)}, bf16[1,128,256]{2,1,0:T(8,128)(2,1)}, u32[]{:S(2)}) copy-start(bf16[1,128,256]{2,1,0:T(8,128)(2,1)} %param.7) | copy-start | bytes 196612
  0.7 0.7 copy-start.14
  1.6 10.2 %copy-start.10 = (f32[1,1,7,16,256]{4,3,2,1,0:T(8,128)S(1)}, f32[1,1,7,16,256]{4,3,2,1,0:T(8,128)}, u32[]{:S(2)}) copy-start(f32[1,1,7,16,256]{4,3,2,1,0:T(8,128)} %param.11) | copy-start | bytes 344068
  3.9 48.0 %all-to-all-start.1 = ((bf16[32,1,6]{2,1,0:T(2,128)(2,1)}), bf16[32,1,6]{2,1,0:T(2,128)(2,1)S(1)}, u32[]{:S(2)}, u32[]{:S(2)}) async-start(bf16[32,1,6]{2,1,0:T(2,128)(2,1)} %all_to_all.12), calls=%async_computation.1 | async-start | bytes 32768 | tf_op jit(solution)/shard_map/all_to_all | solution.py:92
  10.3 0.7 copy-start.13
  11.9 0.9 copy-start.11
  13.4 9.1 %copy-start.12 = (f32[1,32,7,16]{1,3,2,0:T(8,128)S(1)}, f32[1,32,7,16]{1,3,2,0:T(8,128)}, u32[]{:S(2)}) copy-start(f32[1,32,7,16]{1,3,2,0:T(8,128)} %param.12) | copy-start | bytes 43012
  51.9 12.0 %all-to-all-start = ((bf16[32,6,256]{2,1,0:T(8,128)(2,1)}), bf16[32,6,256]{2,1,0:T(8,128)(2,1)S(1)}, u32[]{:S(2)}, u32[]{:S(2)}) async-start(bf16[32,6,256]{2,1,0:T(8,128)(2,1)} %reshape.749), calls=%async_computation | async-start | bytes 262144 | tf_op jit(solution)/shard_map/all_to_all | solution.py:89
  70.9 5.0 %copy-start.8 = (bf16[1,16,64,256]{3,2,1,0:T(8,128)(2,1)S(1)}, bf16[1,16,64,256]{3,2,1,0:T(8,128)(2,1)}, u32[]{:S(2)}) copy-start(bf16[1,16,64,256]{3,2,1,0:T(8,128)(2,1)} %get-tuple-element.123) | copy-start | bytes 1572868
  70.9 5.0 %copy-start.9 = (bf16[1,16,64,256]{3,2,1,0:T(8,128)(2,1)S(1)}, bf16[1,16,64,256]{3,2,1,0:T(8,128)(2,1)}, u32[]{:S(2)}) copy-start(bf16[1,16,64,256]{3,2,1,0:T(8,128)(2,1)} %get-tuple-element.124) | copy-start | bytes 1572868
  71.4 18.9 %collective-permute-start = (f32[256,128]{1,0:T(8,128)S(1)}, f32[256,128]{1,0:T(8,128)S(1)}, u32[]{:S(2)}, u32[]{:S(2)}) collective-permute-start(f32[256,128]{1,0:T(8,128)S(1)} %convolution_bitcast_fusion.6), channel_id=1, source_target_pairs={{3,0},{4,1},{5,2},{6,3},{7,4},{8,5},{9,6},{10,7},{11,8},{12,9},{13... | collective-permute-start | bytes 393224 | tf_op jit(solution)/shard_map/ppermute | solution.py:26
  76.0 3.4 %copy-start.6 = (bf16[1,16,64,256]{3,2,1,0:T(8,128)(2,1)S(1)}, bf16[1,16,64,256]{3,2,1,0:T(8,128)(2,1)}, u32[]{:S(2)}) copy-start(bf16[1,16,64,256]{3,2,1,0:T(8,128)(2,1)} %get-tuple-element.125) | copy-start | bytes 1572868
  76.0 3.4 %copy-start.7 = (bf16[1,16,64,256]{3,2,1,0:T(8,128)(2,1)S(1)}, bf16[1,16,64,256]{3,2,1,0:T(8,128)(2,1)}, u32[]{:S(2)}) copy-start(bf16[1,16,64,256]{3,2,1,0:T(8,128)(2,1)} %get-tuple-element.126) | copy-start | bytes 1572868
  76.5 15.8 %collective-permute-start.1 = (f32[256,128]{1,0:T(8,128)S(1)}, f32[256,128]{1,0:T(8,128)S(1)}, u32[]{:S(2)}, u32[]{:S(2)}) collective-permute-start(f32[256,128]{1,0:T(8,128)S(1)} %convolution_bitcast_fusion.5), channel_id=1, source_target_pairs={{2,0},{3,1},{4,2},{5,3},{6,4},{7,5},{8,6},{9,7},{10,8},{11,9},{12,... | collective-permute-start | bytes 393224 | tf_op jit(solution)/shard_map/ppermute | solution.py:26
  79.4 2.6 %copy-start.4 = (bf16[1,16,64,256]{3,2,1,0:T(8,128)(2,1)S(1)}, bf16[1,16,64,256]{3,2,1,0:T(8,128)(2,1)}, u32[]{:S(2)}) copy-start(bf16[1,16,64,256]{3,2,1,0:T(8,128)(2,1)} %get-tuple-element.127) | copy-start | bytes 1572868
  79.4 2.6 %copy-start.5 = (bf16[1,16,64,256]{3,2,1,0:T(8,128)(2,1)S(1)}, bf16[1,16,64,256]{3,2,1,0:T(8,128)(2,1)}, u32[]{:S(2)}) copy-start(bf16[1,16,64,256]{3,2,1,0:T(8,128)(2,1)} %get-tuple-element.128) | copy-start | bytes 1572868
  79.9 12.4 %collective-permute-start.2 = (f32[256,128]{1,0:T(8,128)S(1)}, f32[256,128]{1,0:T(8,128)S(1)}, u32[]{:S(2)}, u32[]{:S(2)}) collective-permute-start(f32[256,128]{1,0:T(8,128)S(1)} %convolution_bitcast_fusion.4), channel_id=1, source_target_pairs={{1,0},{2,1},{3,2},{4,3},{5,4},{6,5},{7,6},{8,7},{9,8},{10,9},{11,1... | collective-permute-start | bytes 393224 | tf_op jit(solution)/shard_map/ppermute | solution.py:26
  82.0 4.0 %copy-start.2 = (bf16[1,16,64,256]{3,2,1,0:T(8,128)(2,1)S(1)}, bf16[1,16,64,256]{3,2,1,0:T(8,128)(2,1)}, u32[]{:S(2)}) copy-start(bf16[1,16,64,256]{3,2,1,0:T(8,128)(2,1)} %get-tuple-element.129) | copy-start | bytes 1572868
  82.0 4.0 %copy-start.3 = (bf16[1,16,64,256]{3,2,1,0:T(8,128)(2,1)S(1)}, bf16[1,16,64,256]{3,2,1,0:T(8,128)(2,1)}, u32[]{:S(2)}) copy-start(bf16[1,16,64,256]{3,2,1,0:T(8,128)(2,1)} %get-tuple-element.130) | copy-start | bytes 1572868
  82.5 9.8 %collective-permute-start.3 = (f32[256,128]{1,0:T(8,128)S(1)}, f32[256,128]{1,0:T(8,128)S(1)}, u32[]{:S(2)}, u32[]{:S(2)}) collective-permute-start(f32[256,128]{1,0:T(8,128)S(1)} %convolution_bitcast_fusion.2), channel_id=1, source_target_pairs={{0,1},{1,2},{2,3},{3,4},{4,5},{5,6},{6,7},{7,8},{8,9},{9,10},{10,1... | collective-permute-start | bytes 393224 | tf_op jit(solution)/shard_map/ppermute | solution.py:26
  86.0 3.8 %copy-start.1 = (bf16[1,16,64,256]{3,2,1,0:T(8,128)(2,1)S(1)}, bf16[1,16,64,256]{3,2,1,0:T(8,128)(2,1)}, u32[]{:S(2)}) copy-start(bf16[1,16,64,256]{3,2,1,0:T(8,128)(2,1)} %get-tuple-element.132) | copy-start | bytes 1572868
  86.5 9.3 %collective-permute-start.4 = (f32[256,128]{1,0:T(8,128)S(1)}, f32[256,128]{1,0:T(8,128)S(1)}, u32[]{:S(2)}, u32[]{:S(2)}) collective-permute-start(f32[256,128]{1,0:T(8,128)S(1)} %convolution_bitcast_fusion.1), channel_id=1, source_target_pairs={{0,2},{1,3},{2,4},{3,5},{4,6},{5,7},{6,8},{7,9},{8,10},{9,11},{10,... | collective-permute-start | bytes 393224 | tf_op jit(solution)/shard_map/ppermute | solution.py:26
  90.4 8.1 %collective-permute-start.5 = (f32[256,128]{1,0:T(8,128)S(1)}, f32[256,128]{1,0:T(8,128)S(1)}, u32[]{:S(2)}, u32[]{:S(2)}) collective-permute-start(f32[256,128]{1,0:T(8,128)S(1)} %convolution_bitcast_fusion), channel_id=1, source_target_pairs={{0,3},{1,4},{2,5},{3,6},{4,7},{5,8},{6,9},{7,10},{8,11},{9,12},{10... | collective-permute-start | bytes 393224 | tf_op jit(solution)/shard_map/ppermute | solution.py:26
where the time goes:
time: 100 us; the launch traced here: 99.6 us
  other arithmetic  45.8 us (46%)
  starting transfers between devices  30.4 us (30%)
  waiting for transfers between devices  10.9 us (11%)
  local copies, waits for them, and re-layouts  7.65 us (8%)
  matrix products  4.37 us (4%)
    another operation x3, other arithmetic  30.3 us
    ppermute x6, starting transfers between devices, shifted(): return lax.ppermute(shard, axis, pairs)  18.2 us
    convert_element_type x4, other arithmetic, beam_blocks(): ((col_index >= first_col) & (col_index < end_col)).astype(jnp.float32)  8.7 us
    all_to_all x1, starting transfers between devices, shards(): lax.all_to_all(place_slots.reshape(slab_count, CAP), 'slab', split_axis=0...  6.36 us
    ppermute x6, waiting for transfers between devices, shifted(): return lax.ppermute(shard, axis, pairs)  6.13 us
    all_to_all x1, starting transfers between devices, shards(): lax.all_to_all(samples.reshape(slab_count, CAP, NT), 'slab', split_axis=0...  5.83 us
    all_to_all x1, waiting for transfers between devices, shards(): lax.all_to_all(samples.reshape(slab_count, CAP, NT), 'slab', split_axis=0...  4.73 us
    reduce_sum x1, other arithmetic, shards(): beam_re = jnp.sum(spec_re * cosine + spec_im * sine_part, axis=0)  4.72 us
  transfers between devices with their start and end apart: 8, of which 3 were waited for; matrix products, arithmetic and copies ran while one was open for 44% of the time, Pallas kernels for 0%

commit v1 on v0

v1 whole, which is shorter than its diff:
```python
import functools
import math

import jax
import jax.numpy as jnp
import ml_dtypes
import numpy as np
from jax import lax
from jax.experimental import pallas as pl
from jax.experimental.pallas import tpu as pltpu
from jax.sharding import PartitionSpec as P

NT = 256
NF = 64
KLO = 8
P_SIZE = 16
BINS = 16
WIN = 7
XW = 128
HALF = (WIN - 1) // 2
STEPS = NF // KLO
LANES = KLO * P_SIZE

slow_step = 0.25
width_scale = 200.0

ORDER = (3, 2, 4, 1, 5, 0, 6)


def halves(table):
    high = table.astype(ml_dtypes.bfloat16)
    low = (table - high.astype(np.float64)).astype(ml_dtypes.bfloat16)
    return high, low


def dft_halves():
    turns = np.outer(np.arange(NT), np.arange(NF) + KLO) % NT * (2.0 * np.pi / NT)
    return np.concatenate(halves(np.concatenate([np.cos(turns), -np.sin(turns)], axis=1)), axis=1)


def slant_halves():
    omega = (np.arange(NF) + KLO) * (2.0 * np.pi / NT)
    slow = (np.arange(P_SIZE) - (P_SIZE - 1) / 2.0) * slow_step
    place = np.arange(BINS) - (BINS - 1) / 2.0
    phase = place[:, None] * (omega[:, None] * slow[None, :]).reshape(1, -1)
    return np.concatenate(halves(np.concatenate([np.cos(phase), np.sin(phase)], axis=1)), axis=0)


def fit_even(values, degree):
    nodes = 0.125 - 0.125 * np.cos((np.arange(400) + 0.5) * np.pi / 400)
    poly = np.polynomial.chebyshev.Chebyshev.fit(nodes, values(np.sqrt(nodes)), degree, domain=[0, 0.25])
    return [float(c) for c in poly.convert(kind=np.polynomial.Polynomial).coef]


COS_FIT = fit_even(lambda y: np.cos(2 * np.pi * y), 7)
SIN_FIT = fit_even(lambda y: np.sin(2 * np.pi * y) / y, 6)


def horner(fit, s):
    total = jnp.full_like(s, fit[-1])
    for c in fit[-2::-1]:
        total = total * s + c
    return total


def turn(y):
    y = y - jnp.floor(y + 0.5)
    s = y * y
    return horner(COS_FIT, s), horner(SIN_FIT, s) * y


def kernel(
    slabs, scale,
    traces, centre_ids, bins, dft, slant, times, amps, lateral, footprint,
    image,
    spread, sums, send, arrived, ray_t, ray_a, beams, u, v, gauss, step, total,
    send_sem, recv_sem, ray_send, ray_recv, beam_send, beam_recv,
):
    me = lax.axis_index("slab")

    def slab_at(k):
        return lax.rem(me + k, slabs)

    barrier = pltpu.get_barrier_semaphore()

    def greet(k, carry):
        pl.semaphore_signal(barrier, inc=1, device_id={"slab": slab_at(k)}, device_id_type=pl.DeviceIdType.MESH)
        return carry

    lax.fori_loop(1, slabs, greet, 0)

    spectrum = jnp.dot(traces[0], dft[...], preferred_element_type=jnp.float32)
    spectrum = spectrum[:, : 2 * NF] + spectrum[:, 2 * NF :]
    spec_high = spectrum.astype(jnp.bfloat16)
    spec_low = (spectrum - spec_high.astype(jnp.float32)).astype(jnp.bfloat16)
    spec = jnp.concatenate([spec_high, spec_low], axis=1)
    count = spec.shape[0]
    row = lax.broadcasted_iota(jnp.int32, (2 * NF, 2 * NF * P_SIZE), 0)
    column = lax.broadcasted_iota(jnp.int32, (2 * NF, 2 * NF * P_SIZE), 1)
    one_of = jnp.where(row == column // P_SIZE, 1.0, 0.0).astype(jnp.bfloat16)
    spread[: 2 * NF] = one_of
    spread[2 * NF :] = one_of
    bin_row = lax.rem(lax.broadcasted_iota(jnp.int32, (2 * BINS, count), 0), BINS)
    bin_hot = jnp.where(bin_row == bins[...], 1.0, 0.0).T.astype(jnp.bfloat16)
    id_row = lax.broadcasted_iota(jnp.int32, (slabs, count), 0)
    id_hot = jnp.where(id_row == centre_ids[...], 1.0, 0.0)
    id_hot = id_hot.astype(jnp.bfloat16)
    id_hot = jnp.concatenate([id_hot, id_hot], axis=1)
    for chunk in range(STEPS):
        re_at = slice(chunk * LANES, (chunk + 1) * LANES)
        im_at = slice((STEPS + chunk) * LANES, (STEPS + chunk + 1) * LANES)
        spec_re = jnp.dot(spec, spread[:, re_at], preferred_element_type=jnp.float32)
        spec_im = jnp.dot(spec, spread[:, im_at], preferred_element_type=jnp.float32)
        cosine = jnp.dot(bin_hot, slant[:, re_at], preferred_element_type=jnp.float32)
        sine = jnp.dot(bin_hot, slant[:, im_at], preferred_element_type=jnp.float32)
        terms = jnp.concatenate(
            [spec_re * cosine + spec_im * sine, spec_im * cosine - spec_re * sine], axis=1
        )
        high = terms.astype(jnp.bfloat16)
        low = (terms - high.astype(jnp.float32)).astype(jnp.bfloat16)
        partial = jnp.dot(
            id_hot, jnp.concatenate([high, low], axis=0), preferred_element_type=jnp.float32
        )
        sums[:, 2 * chunk, :] = partial[:, :LANES] * scale
        sums[:, 2 * chunk + 1, :] = partial[:, LANES:] * scale
    send[...] = sums[...].astype(jnp.bfloat16)

    pl.semaphore_wait(barrier, slabs - 1)

    def block_copy(k):
        return pltpu.make_async_remote_copy(
            src_ref=send.at[slab_at(k)],
            dst_ref=arrived.at[k],
            send_sem=send_sem.at[k],
            recv_sem=recv_sem.at[k],
            device_id={"slab": slab_at(k)},
            device_id_type=pl.DeviceIdType.MESH,
        )

    def start_block(k, carry):
        block_copy(k).start()
        return carry

    def ray_copies(w):
        target = {"slab": slab_at(slabs + w - HALF)}
        return [
            pltpu.make_async_remote_copy(
                src_ref=source.at[0, 0, w],
                dst_ref=held.at[w],
                send_sem=ray_send.at[i, w],
                recv_sem=ray_recv.at[i, w],
                device_id=target,
                device_id_type=pl.DeviceIdType.MESH,
            )
            for i, (source, held) in enumerate(((times, ray_t), (amps, ray_a)))
        ]

    def beam_copy(w):
        return pltpu.make_async_remote_copy(
            src_ref=beams.at[HALF],
            dst_ref=beams.at[w],
            send_sem=beam_send.at[w],
            recv_sem=beam_recv.at[w],
            device_id={"slab": slab_at(slabs + w - HALF)},
            device_id_type=pl.DeviceIdType.MESH,
        )

    def goes(w):
        target = me + (w - HALF)
        return (target >= 0) & (target < slabs)

    def comes(w):
        source = me - (w - HALF)
        return (source >= 0) & (source < slabs)

    for w in ORDER[1:]:

        @pl.when(goes(w))
        def _():
            for copy in ray_copies(w):
                copy.start()

    lax.fori_loop(1, slabs, start_block, 0)

    def make_u(w, t, a):
        cos8, sin8 = turn(t * (KLO / NT))
        cos1, sin1 = turn(t * (1.0 / NT))
        twice = 2.0 * cos8
        re, im = a, jnp.zeros_like(a)
        for b in range(KLO):
            if b:
                re, im = re * cos1 + im * sin1, im * cos1 - re * sin1
            last_re, last_im = re, im
            now_re, now_im = re * cos8 + im * sin8, im * cos8 - re * sin8
            for chunk in range(STEPS):
                at = 2 * chunk * LANES + b * P_SIZE
                u[w, at : at + P_SIZE, :] = now_re.astype(jnp.bfloat16)
                u[w, at + LANES : at + LANES + P_SIZE, :] = now_im.astype(jnp.bfloat16)
                if chunk < STEPS - 1:
                    now_re, last_re = twice * now_re - last_re, now_re
                    now_im, last_im = twice * now_im - last_im, now_im

    lane = lax.broadcasted_iota(jnp.int32, (1, LANES), 1)
    place = lax.broadcasted_iota(jnp.int32, (XW, LANES), 0)
    rate = -2.0 * math.pi / NT / width_scale * math.log2(math.e)
    rates = (lane // P_SIZE + KLO).astype(jnp.float32) * rate

    def make_gauss(w):
        centre = jnp.clip(me - (w - HALF), 0, slabs - 1)
        axis = lateral[0, centre, w : w + 1, :]
        axis = jnp.concatenate([axis] * KLO, axis=1)
        first, end = footprint[centre, w, 0], footprint[centre, w, 1]
        off = place.astype(jnp.float32) - axis
        off = jnp.where((place >= first) & (place < end), off * off, 1e9)
        gauss[w] = jnp.exp2(off * rates) * (1.0 / math.sqrt(P_SIZE * NF))
        step[w] = jnp.exp2(off * (KLO * rate))

    def add_slot(w):
        here = beams[w].astype(jnp.float32)
        g = gauss[w]
        for chunk in range(STEPS):
            if chunk:
                g = g * step[w]
            at = 2 * chunk * LANES
            v[:, at : at + LANES] = (g * here[2 * chunk : 2 * chunk + 1]).astype(jnp.bfloat16)
            v[:, at + LANES : at + 2 * LANES] = (g * here[2 * chunk + 1 : 2 * chunk + 2]).astype(
                jnp.bfloat16
            )
        return jnp.dot(v[...], u[w], preferred_element_type=jnp.float32)

    make_u(HALF, times[0, 0, HALF], amps[0, 0, HALF])
    for w in ORDER:
        make_gauss(w)
    for w in ORDER[1:]:

        @pl.when(comes(w))
        def _():
            for copy in ray_copies(w):
                copy.wait_recv()
            make_u(w, ray_t[w], ray_a[w])

    def take_block(k, carry):
        block_copy(k).wait_recv()
        return carry + arrived[k].astype(jnp.float32)

    own = lax.fori_loop(1, slabs, take_block, send[me].astype(jnp.float32))
    beams[HALF] = own.astype(jnp.bfloat16)
    for w in ORDER[1:]:

        @pl.when(goes(w))
        def _():
            beam_copy(w).start()

    total[...] = add_slot(HALF)
    for w in ORDER[1:]:

        @pl.when(comes(w))
        def _():
            beam_copy(w).wait_recv()
            total[...] += add_slot(w)

    image[...] = total[...].T

    def sent_block(k, carry):
        block_copy(k).wait_send()
        return carry

    lax.fori_loop(1, slabs, sent_block, 0)
    for w in ORDER[1:]:

        @pl.when(goes(w))
        def _():
            for copy in ray_copies(w):
                copy.wait_send()
            beam_copy(w).wait_send()


def shards(traces, centre_ids, midpoint_bins, ray_times, ray_amps, beam_lateral, footprint):
    slabs = lax.axis_size("slab")
    count = traces.shape[1]
    depth = ray_times.shape[4]
    vmem = pl.BlockSpec(memory_space=pltpu.VMEM)
    smem = pl.BlockSpec(memory_space=pltpu.SMEM)
    partial_image = pl.pallas_call(
        functools.partial(kernel, slabs, 1.0 / math.sqrt(NT * count)),
        out_shape=jax.ShapeDtypeStruct((depth, XW), jnp.float32),
        in_specs=[vmem] * 8 + [smem],
        out_specs=vmem,
        scratch_shapes=[
            pltpu.VMEM((4 * NF, 2 * NF * P_SIZE), jnp.bfloat16),
            pltpu.VMEM((slabs, 2 * STEPS, LANES), jnp.float32),
            pltpu.VMEM((slabs, 2 * STEPS, LANES), jnp.bfloat16),
            pltpu.VMEM((slabs, 2 * STEPS, LANES), jnp.bfloat16),
            pltpu.VMEM((WIN, P_SIZE, depth), jnp.float32),
            pltpu.VMEM((WIN, P_SIZE, depth), jnp.float32),
            pltpu.VMEM((WIN, 2 * STEPS, LANES), jnp.bfloat16),
            pltpu.VMEM((WIN, 2 * NF * P_SIZE, depth), jnp.bfloat16),
            pltpu.VMEM((XW, 2 * NF * P_SIZE), jnp.bfloat16),
            pltpu.VMEM((WIN, XW, LANES), jnp.float32),
            pltpu.VMEM((WIN, XW, LANES), jnp.float32),
            pltpu.VMEM((XW, depth), jnp.float32),
            pltpu.SemaphoreType.DMA((slabs,)),
            pltpu.SemaphoreType.DMA((slabs,)),
            pltpu.SemaphoreType.DMA((2, WIN)),
            pltpu.SemaphoreType.DMA((2, WIN)),
            pltpu.SemaphoreType.DMA((WIN,)),
            pltpu.SemaphoreType.DMA((WIN,)),
        ],
        compiler_params=pltpu.CompilerParams(
            collective_id=0, has_side_effects=True, vmem_limit_bytes=40 * 1024 * 1024
        ),
    )(
        traces,
        centre_ids.reshape(1, count),
        midpoint_bins,
        jnp.asarray(dft_halves()),
        jnp.asarray(slant_halves()),
        ray_times,
        ray_amps,
        beam_lateral,
        footprint,
    )
    if lax.axis_size("offset") == 1:
        return partial_image
    return lax.psum_scatter(partial_image, "offset", scatter_dimension=0, tiled=True)


def solution(mesh):
    return jax.shard_map(
        shards,
        mesh=mesh,
        in_specs=(
            P("offset", "slab", None),
            P("offset", "slab", None),
            P("offset", "slab"),
            P("offset", "slab", None, None, None),
            P("offset", "slab", None, None, None),
            P("offset", None, None, None),
            P(),
        ),
        out_specs=P("offset", "slab"),
        check_vma=False,
    )
```

time: 100 us -> 25.8 us (0.26)
  the two profiles are of different devices: /device:TPU:9 before, /device:TPU:0 now
where the time goes in v1:
time: 25.8 us; the launch traced here: 25.4 us
  Pallas kernels  20.5 us (79%)
  local copies, waits for them, and re-layouts  4.9 us (19%)
    pallas_call x1, Pallas kernels, shards(): pl.pallas_call(functools.partial(kernel, slabs, 1.0 / math.sqrt(NT * coun...  20.5 us
    unnamed x19, local copies, waits for them, and re-layouts  4.9 us

profile of v1, /device:TPU:0, one launch (start us, length us, event | category | flops | bytes accessed | tf_op | source)
XLA Modules:
  0.0 25.4 jit_solution(8049607836745268831)
XLA Ops:
  0.0 0.0 copy-start.7
  0.0 0.0 copy-start
  0.0 0.0 copy-start.1
  0.0 1.0 %copy.10.lateral = f32[1,32,7,16]{3,2,1,0:T(8,128)S(1)} copy(f32[1,32,7,16]{1,3,2,0:T(8,128)} %param.14) | data formatting | bytes 28672 | tf_op args[5]
  1.0 0.0 copy-done.7
  1.0 0.0 copy-start.5
  1.0 0.0 copy-start.6
  1.0 0.1 copy.11.footprint
  1.2 0.0 copy-done
  1.2 0.0 copy-done.1
  1.2 0.5 %copy-done.5 = s32[1,128,1]{1,2,0:T(1,128)S(1)} copy-done((s32[1,128,1]{1,2,0:T(1,128)S(1)}, s32[1,128,1]{1,2,0:T(1,128)}, u32[]{:S(2)}) %copy-start.5) | copy-done | bytes 536
  1.7 0.0 copy-done.6
  1.7 0.0 copy-start.2
  1.7 0.9 %copy-done.2 = f32[1,1,7,16,256]{4,3,2,1,0:T(8,128)S(1)} copy-done((f32[1,1,7,16,256]{4,3,2,1,0:T(8,128)S(1)}, f32[1,1,7,16,256]{4,3,2,1,0:T(8,128)}, u32[]{:S(2)}) %copy-start.2) | copy-done | bytes 114712
  2.6 0.0 copy-start.3
  2.6 0.9 %copy-done.3 = f32[1,1,7,16,256]{4,3,2,1,0:T(8,128)S(1)} copy-done((f32[1,1,7,16,256]{4,3,2,1,0:T(8,128)S(1)}, f32[1,1,7,16,256]{4,3,2,1,0:T(8,128)}, u32[]{:S(2)}) %copy-start.3) | copy-done | bytes 114712
  3.5 0.0 copy-start.4
  3.5 0.8 %copy-done.4 = bf16[1,128,256]{2,1,0:T(8,128)(2,1)S(1)} copy-done((bf16[1,128,256]{2,1,0:T(8,128)(2,1)S(1)}, bf16[1,128,256]{2,1,0:T(8,128)(2,1)}, u32[]{:S(2)}) %copy-start.4) | copy-done | bytes 65560
  4.3 20.5 %shard_map.91 = f32[256,128]{1,0:T(8,128)S(1)} custom-call(bf16[1,128,256]{2,1,0:T(8,128)(2,1)S(1)} %copy-done.4, s32[1,128]{1,0:T(1,128)S(1)} %bitcast.1, s32[1,128]{1,0:T(1,128)S(1)} %copy-done.6, bf16[256,256]{1,0:T(8,128)(2,1)S(1)} %copy-done.1, bf16[32,2048]{1,0:T(8,128)(2,1)S(1)} %copy-done, f32[1,1,7,16,256]{4,3,2,1,0:T(8,128)S(1)} %copy-done.2, ...), custom_call_target="tpu_custom_call" | custom-call | tf_op jit(solution)/shard_map/pallas_call | solution.py:284
  24.8 0.7 %copy.13 = f32[256,128]{1,0:T(8,128)} copy(f32[256,128]{1,0:T(8,128)S(1)} %shard_map.91) | data formatting | bytes 262144
Async XLA Ops:
  0.0 1.0 %copy-start.7 = (s32[32,7,2]{0,2,1:T(2,128)S(1)}, s32[32,7,2]{0,2,1:T(2,128)}, u32[]{:S(2)}) copy-start(s32[32,7,2]{0,2,1:T(2,128)} %param.15) | copy-start | bytes 5380
  0.0 1.2 %copy-start = (bf16[32,2048]{1,0:T(8,128)(2,1)S(1)}, bf16[32,2048]{1,0:T(8,128)(2,1)}, u32[]{:S(2)}) copy-start(bf16[32,2048]{1,0:T(8,128)(2,1)} %constant.5.clone.slant) | copy-start | bytes 393220
  0.0 1.2 %copy-start.1 = (bf16[256,256]{1,0:T(8,128)(2,1)S(1)}, bf16[256,256]{1,0:T(8,128)(2,1)}, u32[]{:S(2)}) copy-start(bf16[256,256]{1,0:T(8,128)(2,1)} %constant.4.clone.dft) | copy-start | bytes 393220
  1.0 0.7 %copy-start.5 = (s32[1,128,1]{1,2,0:T(1,128)S(1)}, s32[1,128,1]{1,2,0:T(1,128)}, u32[]{:S(2)}) copy-start(s32[1,128,1]{1,2,0:T(1,128)} %param.10) | copy-start | bytes 1540
  1.0 0.7 %copy-start.6 = (s32[1,128]{1,0:T(1,128)S(1)}, s32[1,128]{1,0:T(1,128)}, u32[]{:S(2)}) copy-start(s32[1,128]{1,0:T(1,128)} %bins.1) | copy-start | bytes 1540
  1.7 0.9 %copy-start.2 = (f32[1,1,7,16,256]{4,3,2,1,0:T(8,128)S(1)}, f32[1,1,7,16,256]{4,3,2,1,0:T(8,128)}, u32[]{:S(2)}) copy-start(f32[1,1,7,16,256]{4,3,2,1,0:T(8,128)} %times.1) | copy-start | bytes 344068
  2.6 0.9 %copy-start.3 = (f32[1,1,7,16,256]{4,3,2,1,0:T(8,128)S(1)}, f32[1,1,7,16,256]{4,3,2,1,0:T(8,128)}, u32[]{:S(2)}) copy-start(f32[1,1,7,16,256]{4,3,2,1,0:T(8,128)} %amps.1) | copy-start | bytes 344068
  3.5 0.8 %copy-start.4 = (bf16[1,128,256]{2,1,0:T(8,128)(2,1)S(1)}, bf16[1,128,256]{2,1,0:T(8,128)(2,1)}, u32[]{:S(2)}) copy-start(bf16[1,128,256]{2,1,0:T(8,128)(2,1)} %traces.1) | copy-start | bytes 196612

commit v2 on v1

v2 whole, which is shorter than its diff:
```python
import functools
import math

import jax
import jax.numpy as jnp
import ml_dtypes
import numpy as np
from jax import lax
from jax.experimental import pallas as pl
from jax.experimental.pallas import tpu as pltpu
from jax.sharding import PartitionSpec as P

NT = 256
NF = 64
KLO = 8
P_SIZE = 16
BINS = 16
WIN = 7
XW = 128
HALF = (WIN - 1) // 2
STEPS = NF // KLO
LANES = KLO * P_SIZE

slow_step = 0.25
width_scale = 200.0

ORDER = (3, 2, 4, 1, 5, 0, 6)


def halves(table):
    high = table.astype(ml_dtypes.bfloat16)
    low = (table - high.astype(np.float64)).astype(ml_dtypes.bfloat16)
    return high, low


def dft_halves():
    turns = np.outer(np.arange(NT), np.arange(NF) + KLO) % NT * (2.0 * np.pi / NT)
    return np.concatenate(halves(np.concatenate([np.cos(turns), -np.sin(turns)], axis=1)), axis=1)


def by_chunk(table):
    rows = table.shape[0]
    return table.reshape(rows, 2, STEPS, LANES).transpose(0, 2, 1, 3).reshape(rows, -1)


def slant_halves():
    omega = (np.arange(NF) + KLO) * (2.0 * np.pi / NT)
    slow = (np.arange(P_SIZE) - (P_SIZE - 1) / 2.0) * slow_step
    place = np.arange(BINS) - (BINS - 1) / 2.0
    phase = place[:, None] * (omega[:, None] * slow[None, :]).reshape(1, -1)
    table = by_chunk(np.concatenate([np.cos(phase), np.sin(phase)], axis=1))
    return np.concatenate(halves(table), axis=0)


def spread_table():
    one_of = by_chunk(np.repeat(np.eye(2 * NF), P_SIZE, axis=1))
    return np.concatenate([one_of, one_of], axis=0).astype(ml_dtypes.bfloat16)


def fit_even(values, degree):
    nodes = 0.125 - 0.125 * np.cos((np.arange(400) + 0.5) * np.pi / 400)
    poly = np.polynomial.chebyshev.Chebyshev.fit(nodes, values(np.sqrt(nodes)), degree, domain=[0, 0.25])
    return [float(c) for c in poly.convert(kind=np.polynomial.Polynomial).coef]


COS_FIT = fit_even(lambda y: np.cos(2 * np.pi * y), 7)
SIN_FIT = fit_even(lambda y: np.sin(2 * np.pi * y) / y, 6)


def horner(fit, s):
    total = jnp.full_like(s, fit[-1])
    for c in fit[-2::-1]:
        total = total * s + c
    return total


def turn(y):
    y = y - jnp.floor(y + 0.5)
    s = y * y
    return horner(COS_FIT, s), horner(SIN_FIT, s) * y


def kernel(
    slabs, scale,
    traces_in, ids_in, bins_in, dft_in, slant_in, spread_in, times_in, amps_in, lateral_in, footprint_in,
    image,
    traces, ids, bins, dft, slant, spread, lateral, footprint,
    rays, rays_here, sums, send, arrived, beams, u, v, gauss, step,
    load_sem, send_sem, recv_sem, ray_send, ray_recv, beam_send, beam_recv,
):
    me = lax.axis_index("slab")

    def slab_at(k):
        return lax.rem(me + k, slabs)

    loads = [
        pltpu.make_async_copy(source, held, load_sem.at[i])
        for i, (source, held) in enumerate(
            (
                (traces_in.at[0], traces),
                (dft_in, dft),
                (ids_in, ids),
                (bins_in, bins),
                (slant_in, slant),
                (spread_in, spread),
                (times_in.at[0, 0], rays.at[:, 0]),
                (amps_in.at[0, 0], rays.at[:, 1]),
                (lateral_in.at[0], lateral),
                (footprint_in, footprint),
            )
        )
    ]
    for load in loads:
        load.start()

    barrier = pltpu.get_barrier_semaphore()

    def greet(k, carry):
        pl.semaphore_signal(barrier, inc=1, device_id={"slab": slab_at(k)}, device_id_type=pl.DeviceIdType.MESH)
        return carry

    lax.fori_loop(1, slabs, greet, 0)

    def block_copies(first, count):
        return pltpu.make_async_remote_copy(
            src_ref=send.at[pl.ds(slab_at(first), count)] if count == 1 else send.at[pl.ds(0, count)],
            dst_ref=arrived.at[pl.ds(first, count)],
            send_sem=send_sem,
            recv_sem=recv_sem,
            device_id={"slab": slab_at(first)},
            device_id_type=pl.DeviceIdType.MESH,
        )

    def start_block(k, carry):
        block_copies(k, 1).start()
        return carry

    def ray_copy(w):
        return pltpu.make_async_remote_copy(
            src_ref=rays.at[w],
            dst_ref=rays_here.at[w],
            send_sem=ray_send.at[w],
            recv_sem=ray_recv.at[w],
            device_id={"slab": slab_at(slabs + w - HALF)},
            device_id_type=pl.DeviceIdType.MESH,
        )

    def beam_copy(w):
        return pltpu.make_async_remote_copy(
            src_ref=beams.at[HALF],
            dst_ref=beams.at[w],
            send_sem=beam_send.at[w],
            recv_sem=beam_recv.at[w],
            device_id={"slab": slab_at(slabs + w - HALF)},
            device_id_type=pl.DeviceIdType.MESH,
        )

    def goes(w):
        target = me + (w - HALF)
        return (target >= 0) & (target < slabs)

    def comes(w):
        source = me - (w - HALF)
        return (source >= 0) & (source < slabs)

    for load in loads[:4]:
        load.wait()
    spectrum = jnp.dot(traces[...], dft[...], preferred_element_type=jnp.float32)
    spectrum = spectrum[:, : 2 * NF] + spectrum[:, 2 * NF :]
    spec_high = spectrum.astype(jnp.bfloat16)
    spec_low = (spectrum - spec_high.astype(jnp.float32)).astype(jnp.bfloat16)
    spec = jnp.concatenate([spec_high, spec_low], axis=1)
    count = spec.shape[0]
    bin_row = lax.broadcasted_iota(jnp.int32, (2 * BINS, count), 0) % BINS
    bin_hot = jnp.where(bin_row == bins[...], 1.0, 0.0).T.astype(jnp.bfloat16)
    id_row = lax.broadcasted_iota(jnp.int32, (slabs, count), 0)
    id_hot = jnp.where(id_row == ids[...], 1.0, 0.0).astype(jnp.bfloat16)
    id_hot = jnp.concatenate([id_hot, id_hot], axis=1)
    for load in loads[4:8]:
        load.wait()

    pl.semaphore_wait(barrier, slabs - 1)
    for w in ORDER[1:]:

        @pl.when(goes(w))
        def _():
            ray_copy(w).start()

        @pl.when(jnp.logical_not(comes(w)))
        def _():
            rays_here[w] = rays[w]
            beams[w] = jnp.zeros_like(beams[w])

    for chunk in range(STEPS):
        at = slice(2 * chunk * LANES, 2 * (chunk + 1) * LANES)
        spec_wide = jnp.dot(spec, spread[:, at], preferred_element_type=jnp.float32)
        turn_wide = jnp.dot(bin_hot, slant[:, at], preferred_element_type=jnp.float32)
        spec_re, spec_im = spec_wide[:, :LANES], spec_wide[:, LANES:]
        cosine, sine = turn_wide[:, :LANES], turn_wide[:, LANES:]
        terms = jnp.concatenate(
            [spec_re * cosine + spec_im * sine, spec_im * cosine - spec_re * sine], axis=1
        )
        high = terms.astype(jnp.bfloat16)
        low = (terms - high.astype(jnp.float32)).astype(jnp.bfloat16)
        partial = jnp.dot(
            id_hot, jnp.concatenate([high, low], axis=0), preferred_element_type=jnp.float32
        )
        sums[:, 2 * chunk, :] = partial[:, :LANES] * scale
        sums[:, 2 * chunk + 1, :] = partial[:, LANES:] * scale
    send[...] = sums[...].astype(jnp.bfloat16)
    lax.fori_loop(1, slabs, start_block, 0)

    def make_u(w, t, a):
        cos8, sin8 = turn(t * (KLO / NT))
        cos1, sin1 = turn(t * (1.0 / NT))
        twice = 2.0 * cos8
        re, im = a, jnp.zeros_like(a)
        for b in range(KLO):
            if b:
                re, im = re * cos1 + im * sin1, im * cos1 - re * sin1
            last_re, last_im = re, im
            now_re, now_im = re * cos8 + im * sin8, im * cos8 - re * sin8
            for chunk in range(STEPS):
                at = 2 * chunk * LANES + b * P_SIZE
                u[w, at : at + P_SIZE, :] = now_re.astype(jnp.bfloat16)
                u[w, at + LANES : at + LANES + P_SIZE, :] = now_im.astype(jnp.bfloat16)
                if chunk < STEPS - 1:
                    now_re, last_re = twice * now_re - last_re, now_re
                    now_im, last_im = twice * now_im - last_im, now_im

    lane = lax.broadcasted_iota(jnp.int32, (1, LANES), 1)
    place = lax.broadcasted_iota(jnp.int32, (XW, LANES), 0).astype(jnp.float32)
    slow_row = lax.broadcasted_iota(jnp.int32, (P_SIZE, LANES), 0)
    slow_lane = lax.broadcasted_iota(jnp.int32, (P_SIZE, LANES), 1) % P_SIZE
    rate = -2.0 * math.pi / NT / width_scale * math.log2(math.e)
    rates = (lane // P_SIZE + KLO).astype(jnp.float32) * rate

    def pick(values, w):
        centre = jnp.clip(me - (w - HALF), 0, slabs - 1)
        held = lax.broadcasted_iota(jnp.int32, values.shape, 1) == centre
        return jnp.sum(jnp.where(held, values, 0.0), axis=1, keepdims=True)

    def make_gauss(w):
        axis = pick(lateral[w], w)
        axis = jnp.sum(jnp.where(slow_row == slow_lane, axis, 0.0), axis=0, keepdims=True)
        ends = pick(footprint[w].astype(jnp.float32), w)
        off = place - axis
        off = jnp.where((place >= ends[0:1]) & (place < ends[1:2]), off * off, 1e9)
        gauss[w] = jnp.exp2(off * rates) * (1.0 / math.sqrt(P_SIZE * NF))
        step[w] = jnp.exp2(off * (KLO * rate))

    def slot_image(w):
        here = beams[w].astype(jnp.float32)
        g = gauss[w]
        for chunk in range(STEPS):
            if chunk:
                g = g * step[w]
            at = 2 * chunk * LANES
            v[w, :, at : at + LANES] = (g * here[2 * chunk : 2 * chunk + 1]).astype(jnp.bfloat16)
            v[w, :, at + LANES : at + 2 * LANES] = (
                g * here[2 * chunk + 1 : 2 * chunk + 2]
            ).astype(jnp.bfloat16)
        return jnp.dot(v[w], u[w], preferred_element_type=jnp.float32)

    def take_rays(w):
        @pl.when(comes(w))
        def _():
            ray_copy(w).wait_recv()

        make_u(w, rays_here[w, 0], rays_here[w, 1])

    make_u(HALF, rays[HALF, 0], rays[HALF, 1])
    for load in loads[8:]:
        load.wait()
    for w in ORDER:
        make_gauss(w)
    for w in ORDER[1:5]:
        take_rays(w)

    arrived[0] = send[me]
    block_copies(1, slabs - 1).wait_recv()
    own = jnp.sum(arrived[...].astype(jnp.float32), axis=0)
    beams[HALF] = own.astype(jnp.bfloat16)
    for w in ORDER[1:]:

        @pl.when(goes(w))
        def _():
            beam_copy(w).start()

    for w in ORDER[5:]:
        take_rays(w)
    total = slot_image(HALF)
    for w in ORDER[1:]:

        @pl.when(comes(w))
        def _():
            beam_copy(w).wait_recv()

    for w in ORDER[1:]:
        total += slot_image(w)
    image[...] = total.T

    block_copies(1, slabs - 1).wait_send()
    for w in ORDER[1:]:

        @pl.when(goes(w))
        def _():
            ray_copy(w).wait_send()
            beam_copy(w).wait_send()


def shards(traces, centre_ids, midpoint_bins, ray_times, ray_amps, beam_lateral, footprint):
    slabs = lax.axis_size("slab")
    count = traces.shape[1]
    depth = ray_times.shape[4]
    columns = 2 * NF * P_SIZE
    partial_image = pl.pallas_call(
        functools.partial(kernel, slabs, 1.0 / math.sqrt(NT * count)),
        out_shape=jax.ShapeDtypeStruct((depth, XW), jnp.float32),
        in_specs=[pl.BlockSpec(memory_space=pltpu.HBM)] * 10,
        out_specs=pl.BlockSpec(memory_space=pltpu.VMEM),
        scratch_shapes=[
            pltpu.VMEM((count, NT), jnp.bfloat16),
            pltpu.VMEM((1, count), jnp.int32),
            pltpu.VMEM((1, count), jnp.int32),
            pltpu.VMEM((NT, 4 * NF), jnp.bfloat16),
            pltpu.VMEM((2 * BINS, columns), jnp.bfloat16),
            pltpu.VMEM((4 * NF, columns), jnp.bfloat16),
            pltpu.VMEM((WIN, P_SIZE, slabs), jnp.float32),
            pltpu.VMEM((WIN, 2, slabs), jnp.int32),
            pltpu.VMEM((WIN, 2, P_SIZE, depth), jnp.float32),
            pltpu.VMEM((WIN, 2, P_SIZE, depth), jnp.float32),
            pltpu.VMEM((slabs, 2 * STEPS, LANES), jnp.float32),
            pltpu.VMEM((slabs, 2 * STEPS, LANES), jnp.bfloat16),
            pltpu.VMEM((slabs, 2 * STEPS, LANES), jnp.bfloat16),
            pltpu.VMEM((WIN, 2 * STEPS, LANES), jnp.bfloat16),
            pltpu.VMEM((WIN, columns, depth), jnp.bfloat16),
            pltpu.VMEM((WIN, XW, columns), jnp.bfloat16),
            pltpu.VMEM((WIN, XW, LANES), jnp.float32),
            pltpu.VMEM((WIN, XW, LANES), jnp.float32),
            pltpu.SemaphoreType.DMA((10,)),
            pltpu.SemaphoreType.DMA,
            pltpu.SemaphoreType.DMA,
            pltpu.SemaphoreType.DMA((WIN,)),
            pltpu.SemaphoreType.DMA((WIN,)),
            pltpu.SemaphoreType.DMA((WIN,)),
            pltpu.SemaphoreType.DMA((WIN,)),
        ],
        compiler_params=pltpu.CompilerParams(
            collective_id=0, has_side_effects=True, vmem_limit_bytes=63 * 1024 * 1024
        ),
    )(
        traces,
        centre_ids.reshape(1, count),
        midpoint_bins,
        jnp.asarray(dft_halves()),
        jnp.asarray(slant_halves()),
        jnp.asarray(spread_table()),
        ray_times,
        ray_amps,
        beam_lateral.transpose(0, 2, 3, 1),
        footprint.transpose(1, 2, 0),
    )
    if lax.axis_size("offset") == 1:
        return partial_image
    return lax.psum_scatter(partial_image, "offset", scatter_dimension=0, tiled=True)


def solution(mesh):
    return jax.shard_map(
        shards,
        mesh=mesh,
        in_specs=(
            P("offset", "slab", None),
            P("offset", "slab", None),
            P("offset", "slab"),
            P("offset", "slab", None, None, None),
            P("offset", "slab", None, None, None),
            P("offset", None, None, None),
            P(),
        ),
        out_specs=P("offset", "slab"),
        check_vma=False,
    )
```

time: 25.8 us -> 20 us (0.78)
  local copies, waits for them, and re-layouts: 4.9 us -> 1.57 us
  Pallas kernels: 20.5 us -> 18.3 us
    unnamed x19 -> x1, local copies, waits for them, and re-layouts: 4.9 us -> 1.57 us
    pallas_call x1, Pallas kernels: 20.5 us -> 18.3 us  [shards(): pl.pallas_call(functools.partial(kernel, slabs, 1.0 / math.sqrt(NT * coun...]
where the time goes in v2:
time: 20 us; the launch traced here: 19.8 us
  Pallas kernels  18.3 us (92%)
  local copies, waits for them, and re-layouts  1.57 us (8%)
    pallas_call x1, Pallas kernels, shards(): pl.pallas_call(functools.partial(kernel, slabs, 1.0 / math.sqrt(NT * coun...  18.3 us
    unnamed x1, local copies, waits for them, and re-layouts  1.57 us

profile of v2, /device:TPU:0, one launch (start us, length us, event | category | flops | bytes accessed | tf_op | source)
XLA Modules:
  0.0 19.8 jit_solution(18963383864906832)
XLA Ops:
  0.0 18.3 %shard_map.100 = f32[256,128]{1,0:T(8,128)} custom-call(bf16[1,128,256]{2,1,0:T(8,128)(2,1)} %traces_in.1, s32[1,128]{1,0:T(1,128)} %bitcast.5, s32[1,128]{1,0:T(1,128)} %bins_in.1, bf16[256,256]{1,0:T(8,128)(2,1)} %constant.6.clone.dft_in, bf16[32,2048]{1,0:T(8,128)(2,1)} %constant.7.clone.slant_in, bf16[256,2048]{1,0:T(8,128)(2,1)} %constant.8.clone.spread_in, ...), custom_call_target="tpu_custom_call" | custom-call | tf_op jit(solution)/shard_map/pallas_call | solution.py:317
  18.3 1.6 %copy.12 = f32[256,128]{1,0:T(8,128)} copy(f32[256,128]{1,0:T(8,128)} %shard_map.100) | data formatting | bytes 262144

commit v3 on v2

--- a/solution.py
+++ b/solution.py
@@ -40,7 +40,7 @@
 
 def by_chunk(table):
     rows = table.shape[0]
-    return table.reshape(rows, 2, STEPS, LANES).transpose(0, 2, 1, 3).reshape(rows, -1)
+    return table.reshape(rows, 2, STEPS, LANES).transpose(2, 1, 0, 3).reshape(-1, rows, LANES)
 
 
 def slant_halves():
@@ -49,12 +49,12 @@
     place = np.arange(BINS) - (BINS - 1) / 2.0
     phase = place[:, None] * (omega[:, None] * slow[None, :]).reshape(1, -1)
     table = by_chunk(np.concatenate([np.cos(phase), np.sin(phase)], axis=1))
-    return np.concatenate(halves(table), axis=0)
+    return np.concatenate(halves(table), axis=1)
 
 
 def spread_table():
     one_of = by_chunk(np.repeat(np.eye(2 * NF), P_SIZE, axis=1))
-    return np.concatenate([one_of, one_of], axis=0).astype(ml_dtypes.bfloat16)
+    return np.concatenate([one_of, one_of], axis=1).astype(ml_dtypes.bfloat16)
 
 
 def fit_even(values, degree):
@@ -78,6 +78,10 @@
     y = y - jnp.floor(y + 0.5)
     s = y * y
     return horner(COS_FIT, s), horner(SIN_FIT, s) * y
+
+
+def pair(ref, at):
+    return jnp.concatenate([ref[at], ref[at + 1]], axis=1)
 
 
 def kernel(
@@ -89,6 +93,7 @@
     load_sem, send_sem, recv_sem, ray_send, ray_recv, beam_send, beam_recv,
 ):
     me = lax.axis_index("slab")
+    parts = image.shape[0] // 128
 
     def slab_at(k):
         return lax.rem(me + k, slabs)
@@ -192,9 +197,8 @@
             beams[w] = jnp.zeros_like(beams[w])
 
     for chunk in range(STEPS):
-        at = slice(2 * chunk * LANES, 2 * (chunk + 1) * LANES)
-        spec_wide = jnp.dot(spec, spread[:, at], preferred_element_type=jnp.float32)
-        turn_wide = jnp.dot(bin_hot, slant[:, at], preferred_element_type=jnp.float32)
+        spec_wide = jnp.dot(spec, pair(spread, 2 * chunk), preferred_element_type=jnp.float32)
+        turn_wide = jnp.dot(bin_hot, pair(slant, 2 * chunk), preferred_element_type=jnp.float32)
         spec_re, spec_im = spec_wide[:, :LANES], spec_wide[:, LANES:]
         cosine, sine = turn_wide[:, :LANES], turn_wide[:, LANES:]
         terms = jnp.concatenate(
@@ -210,7 +214,12 @@
     send[...] = sums[...].astype(jnp.bfloat16)
     lax.fori_loop(1, slabs, start_block, 0)
 
-    def make_u(w, t, a):
+    def make_u(w, held):
+        for part in range(parts):
+            z = slice(part * 128, (part + 1) * 128)
+            make_u_part(w, part, held[w, 0, :, z], held[w, 1, :, z])
+
+    def make_u_part(w, part, t, a):
         cos8, sin8 = turn(t * (KLO / NT))
         cos1, sin1 = turn(t * (1.0 / NT))
         twice = 2.0 * cos8
@@ -222,8 +231,8 @@
             now_re, now_im = re * cos8 + im * sin8, im * cos8 - re * sin8
             for chunk in range(STEPS):
                 at = 2 * chunk * LANES + b * P_SIZE
-                u[w, at : at + P_SIZE, :] = now_re.astype(jnp.bfloat16)
-                u[w, at + LANES : at + LANES + P_SIZE, :] = now_im.astype(jnp.bfloat16)
+                u[w, part, at : at + P_SIZE, :] = now_re.astype(jnp.bfloat16)
+                u[w, part, at + LANES : at + LANES + P_SIZE, :] = now_im.astype(jnp.bfloat16)
                 if chunk < STEPS - 1:
                     now_re, last_re = twice * now_re - last_re, now_re
                     now_im, last_im = twice * now_im - last_im, now_im
@@ -255,21 +264,22 @@
         for chunk in range(STEPS):
             if chunk:
                 g = g * step[w]
-            at = 2 * chunk * LANES
-            v[w, :, at : at + LANES] = (g * here[2 * chunk : 2 * chunk + 1]).astype(jnp.bfloat16)
-            v[w, :, at + LANES : at + 2 * LANES] = (
-                g * here[2 * chunk + 1 : 2 * chunk + 2]
-            ).astype(jnp.bfloat16)
-        return jnp.dot(v[w], u[w], preferred_element_type=jnp.float32)
+            for at in (2 * chunk, 2 * chunk + 1):
+                v[w, at] = (g * here[at : at + 1]).astype(jnp.bfloat16)
+        return jnp.dot(
+            jnp.concatenate([v[w, at] for at in range(2 * STEPS)], axis=1),
+            jnp.concatenate([u[w, part] for part in range(parts)], axis=1),
+            preferred_element_type=jnp.float32,
+        )
 
     def take_rays(w):
         @pl.when(comes(w))
         def _():
             ray_copy(w).wait_recv()
 
-        make_u(w, rays_here[w, 0], rays_here[w, 1])
-
-    make_u(HALF, rays[HALF, 0], rays[HALF, 1])
+        make_u(w, rays_here)
+
+    make_u(HALF, rays)
     for load in loads[8:]:
         load.wait()
     for w in ORDER:
@@ -314,6 +324,18 @@
     count = traces.shape[1]
     depth = ray_times.shape[4]
     columns = 2 * NF * P_SIZE
+    operands = (
+        traces,
+        centre_ids.reshape(1, count),
+        midpoint_bins,
+        jnp.asarray(dft_halves()),
+        jnp.asarray(slant_halves()),
+        jnp.asarray(spread_table()),
+        ray_times,
+        ray_amps,
+        beam_lateral.transpose(0, 2, 3, 1),
+        footprint.transpose(1, 2, 0),
+    )
     partial_image = pl.pallas_call(
         functools.partial(kernel, slabs, 1.0 / math.sqrt(NT * count)),
         out_shape=jax.ShapeDtypeStruct((depth, XW), jnp.float32),
@@ -324,8 +346,8 @@
             pltpu.VMEM((1, count), jnp.int32),
             pltpu.VMEM((1, count), jnp.int32),
             pltpu.VMEM((NT, 4 * NF), jnp.bfloat16),
-            pltpu.VMEM((2 * BINS, columns), jnp.bfloat16),
-            pltpu.VMEM((4 * NF, columns), jnp.bfloat16),
+            pltpu.VMEM((2 * STEPS, 2 * BINS, LANES), jnp.bfloat16),
+            pltpu.VMEM((2 * STEPS, 4 * NF, LANES), jnp.bfloat16),
             pltpu.VMEM((WIN, P_SIZE, slabs), jnp.float32),
             pltpu.VMEM((WIN, 2, slabs), jnp.int32),
             pltpu.VMEM((WIN, 2, P_SIZE, depth), jnp.float32),
@@ -334,8 +356,8 @@
             pltpu.VMEM((slabs, 2 * STEPS, LANES), jnp.bfloat16),
             pltpu.VMEM((slabs, 2 * STEPS, LANES), jnp.bfloat16),
             pltpu.VMEM((WIN, 2 * STEPS, LANES), jnp.bfloat16),
-            pltpu.VMEM((WIN, columns, depth), jnp.bfloat16),
-            pltpu.VMEM((WIN, XW, columns), jnp.bfloat16),
+            pltpu.VMEM((WIN, depth // 128, columns, 128), jnp.bfloat16),
+            pltpu.VMEM((WIN, 2 * STEPS, XW, LANES), jnp.bfloat16),
             pltpu.VMEM((WIN, XW, LANES), jnp.float32),
             pltpu.VMEM((WIN, XW, LANES), jnp.float32),
             pltpu.SemaphoreType.DMA((10,)),
@@ -347,20 +369,9 @@
             pltpu.SemaphoreType.DMA((WIN,)),
         ],
         compiler_params=pltpu.CompilerParams(
-            collective_id=0, has_side_effects=True, vmem_limit_bytes=63 * 1024 * 1024
+            collective_id=0, has_side_effects=True, vmem_limit_bytes=40 * 1024 * 1024
         ),
-    )(
-        traces,
-        centre_ids.reshape(1, count),
-        midpoint_bins,
-        jnp.asarray(dft_halves()),
-        jnp.asarray(slant_halves()),
-        jnp.asarray(spread_table()),
-        ray_times,
-        ray_amps,
-        beam_lateral.transpose(0, 2, 3, 1),
-        footprint.transpose(1, 2, 0),
-    )
+    )(*[pltpu.with_memory_space_constraint(operand, pltpu.HBM) for operand in operands])
     if lax.axis_size("offset") == 1:
         return partial_image
     return lax.psum_scatter(partial_image, "offset", scatter_dimension=0, tiled=True)

time: 20 us -> 18.5 us (0.925)
  local copies, waits for them, and re-layouts: 1.57 us -> 0.66 us
  Pallas kernels: 18.3 us -> 17.7 us
    unnamed x1, local copies, waits for them, and re-layouts: 1.57 us -> 0.66 us
    pallas_call x1, Pallas kernels: 18.3 us -> 17.7 us  [shards(): pl.pallas_call(functools.partial(kernel, slabs, 1.0 / math.sqrt(NT * coun...]
where the time goes in v3:
time: 18.5 us; the launch traced here: 18.4 us
  Pallas kernels  17.7 us (96%)
  local copies, waits for them, and re-layouts  0.66 us (4%)
    pallas_call x1, Pallas kernels, shards(): pl.pallas_call(functools.partial(kernel, slabs, 1.0 / math.sqrt(NT * coun...  17.7 us
    unnamed x1, local copies, waits for them, and re-layouts  0.66 us

profile of v3, /device:TPU:0, one launch (start us, length us, event | category | flops | bytes accessed | tf_op | source)
XLA Modules:
  0.0 18.4 jit_solution(15477881954666255122)
XLA Ops:
  0.0 17.7 %shard_map.100 = f32[256,128]{1,0:T(8,128)S(1)} custom-call(bf16[1,128,256]{2,1,0:T(8,128)(2,1)} %traces_in.1, s32[1,128]{1,0:T(1,128)} %bitcast.5, s32[1,128]{1,0:T(1,128)} %bins_in.1, bf16[256,256]{1,0:T(8,128)(2,1)} %constant.6.clone.dft_in, bf16[16,32,128]{2,1,0:T(8,128)(2,1)} %constant.7.clone.slant_in, bf16[16,256,128]{2,1,0:T(8,128)(2,1)} %constant.8.clone.spread_in, ...), custom_call_target="tpu_custom_call" | custom-call | tf_op jit(solution)/shard_map/pallas_call | solution.py:339
  17.7 0.7 %copy.12 = f32[256,128]{1,0:T(8,128)} copy(f32[256,128]{1,0:T(8,128)S(1)} %shard_map.100) | data formatting | bytes 262144

commit v4 on v3

--- a/solution.py
+++ b/solution.py
@@ -24,7 +24,11 @@
 slow_step = 0.25
 width_scale = 200.0
 
-ORDER = (3, 2, 4, 1, 5, 0, 6)
+def order(i):
+    return HALF + (i + 1) // 2 * (1 - 2 * (i % 2))
+
+
+OTHERS = [order(i) for i in range(1, WIN)]
 
 
 def halves(table):
@@ -89,7 +93,7 @@
     traces_in, ids_in, bins_in, dft_in, slant_in, spread_in, times_in, amps_in, lateral_in, footprint_in,
     image,
     traces, ids, bins, dft, slant, spread, lateral, footprint,
-    rays, rays_here, sums, send, arrived, beams, u, v, gauss, step,
+    rays, rays_here, sums, send, arrived, beams, u, v, gauss, step, total,
     load_sem, send_sem, recv_sem, ray_send, ray_recv, beam_send, beam_recv,
 ):
     me = lax.axis_index("slab")
@@ -185,7 +189,7 @@
         load.wait()
 
     pl.semaphore_wait(barrier, slabs - 1)
-    for w in ORDER[1:]:
+    for w in OTHERS:
 
         @pl.when(goes(w))
         def _():
@@ -249,7 +253,7 @@
         held = lax.broadcasted_iota(jnp.int32, values.shape, 1) == centre
         return jnp.sum(jnp.where(held, values, 0.0), axis=1, keepdims=True)
 
-    def make_gauss(w):
+    def make_gauss(w, carry):
         axis = pick(lateral[w], w)
         axis = jnp.sum(jnp.where(slow_row == slow_lane, axis, 0.0), axis=0, keepdims=True)
         ends = pick(footprint[w].astype(jnp.float32), w)
@@ -257,6 +261,7 @@
         off = jnp.where((place >= ends[0:1]) & (place < ends[1:2]), off * off, 1e9)
         gauss[w] = jnp.exp2(off * rates) * (1.0 / math.sqrt(P_SIZE * NF))
         step[w] = jnp.exp2(off * (KLO * rate))
+        return carry
 
     def slot_image(w):
         here = beams[w].astype(jnp.float32)
@@ -272,46 +277,50 @@
             preferred_element_type=jnp.float32,
         )
 
-    def take_rays(w):
-        @pl.when(comes(w))
+    def take_rays(i, carry):
+        w = order(i)
+
+        @pl.when(comes(w) & (w != HALF))
         def _():
             ray_copy(w).wait_recv()
 
         make_u(w, rays_here)
-
-    make_u(HALF, rays)
+        return carry
+
+    rays_here[HALF] = rays[HALF]
     for load in loads[8:]:
         load.wait()
-    for w in ORDER:
-        make_gauss(w)
-    for w in ORDER[1:5]:
-        take_rays(w)
+    lax.fori_loop(0, WIN, make_gauss, 0)
+    lax.fori_loop(0, 5, take_rays, 0)
 
     arrived[0] = send[me]
     block_copies(1, slabs - 1).wait_recv()
     own = jnp.sum(arrived[...].astype(jnp.float32), axis=0)
     beams[HALF] = own.astype(jnp.bfloat16)
-    for w in ORDER[1:]:
+    for w in OTHERS:
 
         @pl.when(goes(w))
         def _():
             beam_copy(w).start()
 
-    for w in ORDER[5:]:
-        take_rays(w)
-    total = slot_image(HALF)
-    for w in ORDER[1:]:
-
-        @pl.when(comes(w))
+    lax.fori_loop(5, WIN, take_rays, 0)
+    total[...] = jnp.zeros_like(total)
+
+    def add_slot(i, carry):
+        w = order(i)
+
+        @pl.when(comes(w) & (w != HALF))
         def _():
             beam_copy(w).wait_recv()
 
-    for w in ORDER[1:]:
-        total += slot_image(w)
-    image[...] = total.T
+        total[...] += slot_image(w)
+        return carry
+
+    lax.fori_loop(0, WIN, add_slot, 0)
+    image[...] = total[...].T
 
     block_copies(1, slabs - 1).wait_send()
-    for w in ORDER[1:]:
+    for w in OTHERS:
 
         @pl.when(goes(w))
         def _():
@@ -360,6 +369,7 @@
             pltpu.VMEM((WIN, 2 * STEPS, XW, LANES), jnp.bfloat16),
             pltpu.VMEM((WIN, XW, LANES), jnp.float32),
             pltpu.VMEM((WIN, XW, LANES), jnp.float32),
+            pltpu.VMEM((XW, depth), jnp.float32),
             pltpu.SemaphoreType.DMA((10,)),
             pltpu.SemaphoreType.DMA,
             pltpu.SemaphoreType.DMA,

time: 18.5 us -> 18.6 us (level)
  no operation moved by 1% of the time
where the time goes in v4:
time: 18.6 us; the launch traced here: 18.4 us
  Pallas kernels  17.8 us (96%)
  local copies, waits for them, and re-layouts  0.66 us (4%)
    pallas_call x1, Pallas kernels, shards(): pl.pallas_call(functools.partial(kernel, slabs, 1.0 / math.sqrt(NT * coun...  17.8 us
    unnamed x1, local copies, waits for them, and re-layouts  0.66 us

profile of v4, /device:TPU:0, one launch (start us, length us, event | category | flops | bytes accessed | tf_op | source)
XLA Modules:
  0.0 18.4 jit_solution(10698360153205967512)
XLA Ops:
  0.0 17.8 %shard_map.100 = f32[256,128]{1,0:T(8,128)S(1)} custom-call(bf16[1,128,256]{2,1,0:T(8,128)(2,1)} %traces_in.1, s32[1,128]{1,0:T(1,128)} %bitcast.5, s32[1,128]{1,0:T(1,128)} %bins_in.1, bf16[256,256]{1,0:T(8,128)(2,1)} %constant.6.clone.dft_in, bf16[16,32,128]{2,1,0:T(8,128)(2,1)} %constant.7.clone.slant_in, bf16[16,256,128]{2,1,0:T(8,128)(2,1)} %constant.8.clone.spread_in, ...), custom_call_target="tpu_custom_call" | custom-call | tf_op jit(solution)/shard_map/pallas_call | solution.py:348
  17.8 0.7 %copy.12 = f32[256,128]{1,0:T(8,128)} copy(f32[256,128]{1,0:T(8,128)S(1)} %shard_map.100) | data formatting | bytes 262144

commit v5 on v4

--- a/solution.py
+++ b/solution.py
@@ -38,8 +38,9 @@
 
 
 def dft_halves():
-    turns = np.outer(np.arange(NT), np.arange(NF) + KLO) % NT * (2.0 * np.pi / NT)
-    return np.concatenate(halves(np.concatenate([np.cos(turns), -np.sin(turns)], axis=1)), axis=1)
+    turns = np.outer(np.arange(NF) + KLO, np.arange(NT)) % NT * (2.0 * np.pi / NT)
+    table = np.stack([np.cos(turns), -np.sin(turns)]).reshape(2, STEPS, KLO, NT)
+    return np.concatenate(halves(table.transpose(1, 0, 2, 3).reshape(2 * NF, NT)), axis=0)
 
 
 def by_chunk(table):
@@ -57,7 +58,7 @@
 
 
 def spread_table():
-    one_of = by_chunk(np.repeat(np.eye(2 * NF), P_SIZE, axis=1))
+    one_of = np.repeat(np.eye(2 * KLO), P_SIZE, axis=1).reshape(2 * KLO, 2, LANES).transpose(1, 0, 2)
     return np.concatenate([one_of, one_of], axis=1).astype(ml_dtypes.bfloat16)
 
 
@@ -172,14 +173,22 @@
         source = me - (w - HALF)
         return (source >= 0) & (source < slabs)
 
+    def send_rays(slots):
+        for w in slots:
+
+            @pl.when(goes(w))
+            def _():
+                ray_copy(w).start()
+
     for load in loads[:4]:
         load.wait()
-    spectrum = jnp.dot(traces[...], dft[...], preferred_element_type=jnp.float32)
-    spectrum = spectrum[:, : 2 * NF] + spectrum[:, 2 * NF :]
+    spectrum = lax.dot_general(
+        dft[...], traces[...], (((1,), (1,)), ((), ())), preferred_element_type=jnp.float32
+    )
+    spectrum = spectrum[: 2 * NF] + spectrum[2 * NF :]
     spec_high = spectrum.astype(jnp.bfloat16)
     spec_low = (spectrum - spec_high.astype(jnp.float32)).astype(jnp.bfloat16)
-    spec = jnp.concatenate([spec_high, spec_low], axis=1)
-    count = spec.shape[0]
+    count = spectrum.shape[1]
     bin_row = lax.broadcasted_iota(jnp.int32, (2 * BINS, count), 0) % BINS
     bin_hot = jnp.where(bin_row == bins[...], 1.0, 0.0).T.astype(jnp.bfloat16)
     id_row = lax.broadcasted_iota(jnp.int32, (slabs, count), 0)
@@ -189,19 +198,21 @@
         load.wait()
 
     pl.semaphore_wait(barrier, slabs - 1)
+    send_rays(OTHERS[:2])
     for w in OTHERS:
-
-        @pl.when(goes(w))
-        def _():
-            ray_copy(w).start()
 
         @pl.when(jnp.logical_not(comes(w)))
         def _():
             rays_here[w] = rays[w]
             beams[w] = jnp.zeros_like(beams[w])
 
+    spread_wide = pair(spread, 0)
     for chunk in range(STEPS):
-        spec_wide = jnp.dot(spec, pair(spread, 2 * chunk), preferred_element_type=jnp.float32)
+        rows = slice(2 * chunk * KLO, 2 * (chunk + 1) * KLO)
+        spec = jnp.concatenate([spec_high[rows], spec_low[rows]], axis=0)
+        spec_wide = lax.dot_general(
+            spec, spread_wide, (((0,), (0,)), ((), ())), preferred_element_type=jnp.float32
+        )
         turn_wide = jnp.dot(bin_hot, pair(slant, 2 * chunk), preferred_element_type=jnp.float32)
         spec_re, spec_im = spec_wide[:, :LANES], spec_wide[:, LANES:]
         cosine, sine = turn_wide[:, :LANES], turn_wide[:, LANES:]
@@ -217,6 +228,7 @@
         sums[:, 2 * chunk + 1, :] = partial[:, LANES:] * scale
     send[...] = sums[...].astype(jnp.bfloat16)
     lax.fori_loop(1, slabs, start_block, 0)
+    send_rays(OTHERS[2:])
 
     def make_u(w, held):
         for part in range(parts):
@@ -354,9 +366,9 @@
             pltpu.VMEM((count, NT), jnp.bfloat16),
             pltpu.VMEM((1, count), jnp.int32),
             pltpu.VMEM((1, count), jnp.int32),
-            pltpu.VMEM((NT, 4 * NF), jnp.bfloat16),
+            pltpu.VMEM((4 * NF, NT), jnp.bfloat16),
             pltpu.VMEM((2 * STEPS, 2 * BINS, LANES), jnp.bfloat16),
-            pltpu.VMEM((2 * STEPS, 4 * NF, LANES), jnp.bfloat16),
+            pltpu.VMEM((2, 4 * KLO, LANES), jnp.bfloat16),
             pltpu.VMEM((WIN, P_SIZE, slabs), jnp.float32),
             pltpu.VMEM((WIN, 2, slabs), jnp.int32),
             pltpu.VMEM((WIN, 2, P_SIZE, depth), jnp.float32),

time: 18.6 us -> 19.2 us (1.032)
  Pallas kernels: 17.8 us -> 18.4 us
    pallas_call x1, Pallas kernels: 17.8 us -> 18.4 us  [shards(): pl.pallas_call(functools.partial(kernel, slabs, 1.0 / math.sqrt(NT * coun...]
where the time goes in v5:
time: 19.2 us; the launch traced here: 19 us
  Pallas kernels  18.4 us (96%)
  local copies, waits for them, and re-layouts  0.66 us (3%)
    pallas_call x1, Pallas kernels, shards(): pl.pallas_call(functools.partial(kernel, slabs, 1.0 / math.sqrt(NT * coun...  18.4 us
    unnamed x1, local copies, waits for them, and re-layouts  0.66 us

profile of v5, /device:TPU:0, one launch (start us, length us, event | category | flops | bytes accessed | tf_op | source)
XLA Modules:
  0.0 19.0 jit_solution(12500064525042024861)
XLA Ops:
  0.0 18.4 %shard_map.100 = f32[256,128]{1,0:T(8,128)S(1)} custom-call(bf16[1,128,256]{2,1,0:T(8,128)(2,1)} %traces_in.1, s32[1,128]{1,0:T(1,128)} %bitcast.5, s32[1,128]{1,0:T(1,128)} %bins_in.1, bf16[256,256]{1,0:T(8,128)(2,1)} %constant.6.clone.dft_in, bf16[16,32,128]{2,1,0:T(8,128)(2,1)} %constant.7.clone.slant_in, bf16[2,32,128]{2,1,0:T(8,128)(2,1)} %constant.8.clone.spread_in, ...), custom_call_target="tpu_custom_call" | custom-call | tf_op jit(solution)/shard_map/pallas_call | solution.py:360
  18.4 0.7 %copy.12 = f32[256,128]{1,0:T(8,128)} copy(f32[256,128]{1,0:T(8,128)S(1)} %shard_map.100) | data formatting | bytes 262144

commit v6 on v5

--- a/solution.py
+++ b/solution.py
@@ -92,13 +92,13 @@
 def kernel(
     slabs, scale,
     traces_in, ids_in, bins_in, dft_in, slant_in, spread_in, times_in, amps_in, lateral_in, footprint_in,
-    image,
+    u, gauss, step, beams,
     traces, ids, bins, dft, slant, spread, lateral, footprint,
-    rays, rays_here, sums, send, arrived, beams, u, v, gauss, step, total,
+    rays, rays_here, sums, send, arrived,
     load_sem, send_sem, recv_sem, ray_send, ray_recv, beam_send, beam_recv,
 ):
     me = lax.axis_index("slab")
-    parts = image.shape[0] // 128
+    parts = u.shape[1]
 
     def slab_at(k):
         return lax.rem(me + k, slabs)
@@ -198,7 +198,7 @@
         load.wait()
 
     pl.semaphore_wait(barrier, slabs - 1)
-    send_rays(OTHERS[:2])
+    send_rays(OTHERS)
     for w in OTHERS:
 
         @pl.when(jnp.logical_not(comes(w)))
@@ -228,7 +228,6 @@
         sums[:, 2 * chunk + 1, :] = partial[:, LANES:] * scale
     send[...] = sums[...].astype(jnp.bfloat16)
     lax.fori_loop(1, slabs, start_block, 0)
-    send_rays(OTHERS[2:])
 
     def make_u(w, held):
         for part in range(parts):
@@ -275,7 +274,51 @@
         step[w] = jnp.exp2(off * (KLO * rate))
         return carry
 
-    def slot_image(w):
+    def take_rays(i, carry):
+        w = order(i)
+
+        @pl.when(comes(w) & (w != HALF))
+        def _():
+            ray_copy(w).wait_recv()
+
+        make_u(w, rays_here)
+        return carry
+
+    rays_here[HALF] = rays[HALF]
+    for load in loads[8:]:
+        load.wait()
+    lax.fori_loop(0, WIN, make_gauss, 0)
+    lax.fori_loop(0, 5, take_rays, 0)
+
+    arrived[0] = send[me]
+    block_copies(1, slabs - 1).wait_recv()
+    own = jnp.sum(arrived[...].astype(jnp.float32), axis=0)
+    beams[HALF] = own.astype(jnp.bfloat16)
+    for w in OTHERS:
+
+        @pl.when(goes(w))
+        def _():
+            beam_copy(w).start()
+
+    lax.fori_loop(5, WIN, take_rays, 0)
+    for w in OTHERS:
+
+        @pl.when(comes(w))
+        def _():
+            beam_copy(w).wait_recv()
+
+    block_copies(1, slabs - 1).wait_send()
+    for w in OTHERS:
+
+        @pl.when(goes(w))
+        def _():
+            ray_copy(w).wait_send()
+            beam_copy(w).wait_send()
+
+
+def image_kernel(u, gauss, step, beams, image, v):
+    total = jnp.zeros((XW, image.shape[0]), jnp.float32)
+    for w in range(WIN):
         here = beams[w].astype(jnp.float32)
         g = gauss[w]
         for chunk in range(STEPS):
@@ -283,61 +326,12 @@
                 g = g * step[w]
             for at in (2 * chunk, 2 * chunk + 1):
                 v[w, at] = (g * here[at : at + 1]).astype(jnp.bfloat16)
-        return jnp.dot(
+        total += jnp.dot(
             jnp.concatenate([v[w, at] for at in range(2 * STEPS)], axis=1),
-            jnp.concatenate([u[w, part] for part in range(parts)], axis=1),
+            jnp.concatenate([u[w, part] for part in range(u.shape[1])], axis=1),
             preferred_element_type=jnp.float32,
         )
-
-    def take_rays(i, carry):
-        w = order(i)
-
-        @pl.when(comes(w) & (w != HALF))
-        def _():
-            ray_copy(w).wait_recv()
-
-        make_u(w, rays_here)
-        return carry
-
-    rays_here[HALF] = rays[HALF]
-    for load in loads[8:]:
-        load.wait()
-    lax.fori_loop(0, WIN, make_gauss, 0)
-    lax.fori_loop(0, 5, take_rays, 0)
-
-    arrived[0] = send[me]
-    block_copies(1, slabs - 1).wait_recv()
-    own = jnp.sum(arrived[...].astype(jnp.float32), axis=0)
-    beams[HALF] = own.astype(jnp.bfloat16)
-    for w in OTHERS:
-
-        @pl.when(goes(w))
-        def _():
-            beam_copy(w).start()
-
-    lax.fori_loop(5, WIN, take_rays, 0)
-    total[...] = jnp.zeros_like(total)
-
-    def add_slot(i, carry):
-        w = order(i)
-
-        @pl.when(comes(w) & (w != HALF))
-        def _():
-            beam_copy(w).wait_recv()
-
-        total[...] += slot_image(w)
-        return carry
-
-    lax.fori_loop(0, WIN, add_slot, 0)
-    image[...] = total[...].T
-
-    block_copies(1, slabs - 1).wait_send()
-    for w in OTHERS:
-
-        @pl.when(goes(w))
-        def _():
-            ray_copy(w).wait_send()
-            beam_copy(w).wait_send()
+    image[...] = total.T
 
 
 def shards(traces, centre_ids, midpoint_bins, ray_times, ray_amps, beam_lateral, footprint):
@@ -357,11 +351,17 @@
         beam_lateral.transpose(0, 2, 3, 1),
         footprint.transpose(1, 2, 0),
     )
-    partial_image = pl.pallas_call(
+    vmem = pl.BlockSpec(memory_space=pltpu.VMEM)
+    tables = pl.pallas_call(
         functools.partial(kernel, slabs, 1.0 / math.sqrt(NT * count)),
-        out_shape=jax.ShapeDtypeStruct((depth, XW), jnp.float32),
+        out_shape=[
+            jax.ShapeDtypeStruct((WIN, depth // 128, columns, 128), jnp.bfloat16),
+            jax.ShapeDtypeStruct((WIN, XW, LANES), jnp.float32),
+            jax.ShapeDtypeStruct((WIN, XW, LANES), jnp.float32),
+            jax.ShapeDtypeStruct((WIN, 2 * STEPS, LANES), jnp.bfloat16),
+        ],
         in_specs=[pl.BlockSpec(memory_space=pltpu.HBM)] * 10,
-        out_specs=pl.BlockSpec(memory_space=pltpu.VMEM),
+        out_specs=[vmem] * 4,
         scratch_shapes=[
             pltpu.VMEM((count, NT), jnp.bfloat16),
             pltpu.VMEM((1, count), jnp.int32),
@@ -376,12 +376,6 @@
             pltpu.VMEM((slabs, 2 * STEPS, LANES), jnp.float32),
             pltpu.VMEM((slabs, 2 * STEPS, LANES), jnp.bfloat16),
             pltpu.VMEM((slabs, 2 * STEPS, LANES), jnp.bfloat16),
-            pltpu.VMEM((WIN, 2 * STEPS, LANES), jnp.bfloat16),
-            pltpu.VMEM((WIN, depth // 128, columns, 128), jnp.bfloat16),
-            pltpu.VMEM((WIN, 2 * STEPS, XW, LANES), jnp.bfloat16),
-            pltpu.VMEM((WIN, XW, LANES), jnp.float32),
-            pltpu.VMEM((WIN, XW, LANES), jnp.float32),
-            pltpu.VMEM((XW, depth), jnp.float32),
             pltpu.SemaphoreType.DMA((10,)),
             pltpu.SemaphoreType.DMA,
             pltpu.SemaphoreType.DMA,
@@ -391,9 +385,17 @@
             pltpu.SemaphoreType.DMA((WIN,)),
         ],
         compiler_params=pltpu.CompilerParams(
-            collective_id=0, has_side_effects=True, vmem_limit_bytes=40 * 1024 * 1024
+            collective_id=0, has_side_effects=True, vmem_limit_bytes=24 * 1024 * 1024
         ),
     )(*[pltpu.with_memory_space_constraint(operand, pltpu.HBM) for operand in operands])
+    partial_image = pl.pallas_call(
+        image_kernel,
+        out_shape=jax.ShapeDtypeStruct((depth, XW), jnp.float32),
+        in_specs=[vmem] * 4,
+        out_specs=vmem,
+        scratch_shapes=[pltpu.VMEM((WIN, 2 * STEPS, XW, LANES), jnp.bfloat16)],
+        compiler_params=pltpu.CompilerParams(vmem_limit_bytes=24 * 1024 * 1024),
+    )(*tables)
     if lax.axis_size("offset") == 1:
         return partial_image
     return lax.psum_scatter(partial_image, "offset", scatter_dimension=0, tiled=True)

time: 19.2 us -> 18.8 us (0.979)
  local copies, waits for them, and re-layouts: 0.66 us -> 0 us
  Pallas kernels: 18.4 us -> 18.6 us
    pallas_call x0 -> x1, Pallas kernels: none -> 2.4 us  [shards(): pl.pallas_call(image_kernel, out_shape=jax.ShapeDtypeStruct((depth, XW),...]
    pallas_call x1, Pallas kernels: 18.4 us -> 16.2 us  [shards(): pl.pallas_call(functools.partial(kernel, slabs, 1.0 / math.sqrt(NT * coun...]
    unnamed x1 -> x0, local copies, waits for them, and re-layouts: 0.66 us -> none
where the time goes in v6:
time: 18.8 us; the launch traced here: 18.6 us
  Pallas kernels  18.6 us (99%)
    pallas_call x1, Pallas kernels, shards(): pl.pallas_call(functools.partial(kernel, slabs, 1.0 / math.sqrt(NT * coun...  16.2 us
    pallas_call x1, Pallas kernels, shards(): pl.pallas_call(image_kernel, out_shape=jax.ShapeDtypeStruct((depth, XW),...  2.4 us

profile of v6, /device:TPU:0, one launch (start us, length us, event | category | flops | bytes accessed | tf_op | source)
XLA Modules:
  0.0 18.6 jit_solution(18178001638672164018)
XLA Ops:
  0.0 16.2 %shard_map.100 = (bf16[7,2,2048,128]{3,2,1,0:T(8,128)(2,1)S(1)}, f32[7,128,128]{2,1,0:T(8,128)S(1)}, f32[7,128,128]{2,1,0:T(8,128)S(1)}, bf16[7,16,128]{2,1,0:T(8,128)(2,1)S(1)}) custom-call(bf16[1,128,256]{2,1,0:T(8,128)(2,1)} %traces_in.1, s32[1,128]{1,0:T(1,128)} %bitcast.5, s32[1,128]{1,0:T(1,128)} %bins_in.1, bf16[256,256]{1,0:T(8,128)(2,1)} %constant.6.clone.dft_in, ...), custom_call_target="tpu_custom_call" | custom-call | tf_op jit(solution)/shard_map/pallas_call | solution.py:355
  16.2 2.4 %shard_map.101 = f32[256,128]{1,0:T(8,128)} custom-call(bf16[7,2,2048,128]{3,2,1,0:T(8,128)(2,1)S(1)} %get-tuple-element.9.u, f32[7,128,128]{2,1,0:T(8,128)S(1)} %get-tuple-element.10.gauss, f32[7,128,128]{2,1,0:T(8,128)S(1)} %get-tuple-element.11.step, bf16[7,16,128]{2,1,0:T(8,128)(2,1)S(1)} %get-tuple-element.12.beams), custom_call_target="tpu_custom_call" | custom-call | tf_op jit(solution)/shard_map/pallas_call | solution.py:391

commit v7 on v6

--- a/solution.py
+++ b/solution.py
@@ -20,6 +20,7 @@
 HALF = (WIN - 1) // 2
 STEPS = NF // KLO
 LANES = KLO * P_SIZE
+GROUP = 8
 
 slow_step = 0.25
 width_scale = 200.0
@@ -38,9 +39,8 @@
 
 
 def dft_halves():
-    turns = np.outer(np.arange(NF) + KLO, np.arange(NT)) % NT * (2.0 * np.pi / NT)
-    table = np.stack([np.cos(turns), -np.sin(turns)]).reshape(2, STEPS, KLO, NT)
-    return np.concatenate(halves(table.transpose(1, 0, 2, 3).reshape(2 * NF, NT)), axis=0)
+    turns = np.outer(np.arange(NT), np.arange(NF) + KLO) % NT * (2.0 * np.pi / NT)
+    return np.concatenate(halves(np.concatenate([np.cos(turns), -np.sin(turns)], axis=1)), axis=1)
 
 
 def by_chunk(table):
@@ -58,8 +58,7 @@
 
 
 def spread_table():
-    one_of = np.repeat(np.eye(2 * KLO), P_SIZE, axis=1).reshape(2 * KLO, 2, LANES).transpose(1, 0, 2)
-    return np.concatenate([one_of, one_of], axis=1).astype(ml_dtypes.bfloat16)
+    return by_chunk(np.repeat(np.eye(2 * NF), P_SIZE, axis=1)).astype(ml_dtypes.bfloat16)
 
 
 def fit_even(values, degree):
@@ -94,14 +93,33 @@
     traces_in, ids_in, bins_in, dft_in, slant_in, spread_in, times_in, amps_in, lateral_in, footprint_in,
     u, gauss, step, beams,
     traces, ids, bins, dft, slant, spread, lateral, footprint,
-    rays, rays_here, sums, send, arrived,
-    load_sem, send_sem, recv_sem, ray_send, ray_recv, beam_send, beam_recv,
+    rays, rays_here, sums, send, arrived, group_sum, group_send, group_arrived,
+    load_sem, send_sem, recv_sem, peer_send, peer_recv, ray_send, ray_recv, beam_send, beam_recv,
 ):
     me = lax.axis_index("slab")
     parts = u.shape[1]
 
     def slab_at(k):
         return lax.rem(me + k, slabs)
+
+    def goes(w):
+        target = me + (w - HALF)
+        return (target >= 0) & (target < slabs)
+
+    def comes(w):
+        source = me - (w - HALF)
+        return (source >= 0) & (source < slabs)
+
+    groups = slabs // GROUP
+    group = me // GROUP
+    base = group * GROUP
+    spot = lax.rem(me, GROUP)
+
+    def mate(k):
+        return base + lax.rem(spot + k, GROUP)
+
+    def peer(k):
+        return lax.rem(group + k, groups) * GROUP + spot
 
     loads = [
         pltpu.make_async_copy(source, held, load_sem.at[i])
@@ -125,25 +143,43 @@
 
     barrier = pltpu.get_barrier_semaphore()
 
-    def greet(k, carry):
-        pl.semaphore_signal(barrier, inc=1, device_id={"slab": slab_at(k)}, device_id_type=pl.DeviceIdType.MESH)
-        return carry
-
-    lax.fori_loop(1, slabs, greet, 0)
-
-    def block_copies(first, count):
+    def greet(target):
+        pl.semaphore_signal(
+            barrier, inc=1, device_id={"slab": target}, device_id_type=pl.DeviceIdType.MESH
+        )
+
+    for k in range(1, GROUP):
+        greet(mate(k))
+    for k in range(1, groups):
+        greet(peer(k))
+    greetings = GROUP - 1 + groups - 1
+    for w in OTHERS:
+
+        @pl.when(goes(w))
+        def _():
+            greet(slab_at(slabs + w - HALF))
+
+        greetings = greetings + jnp.where(goes(w), 1, 0)
+
+    def mate_copy(k):
         return pltpu.make_async_remote_copy(
-            src_ref=send.at[pl.ds(slab_at(first), count)] if count == 1 else send.at[pl.ds(0, count)],
-            dst_ref=arrived.at[pl.ds(first, count)],
-            send_sem=send_sem,
-            recv_sem=recv_sem,
-            device_id={"slab": slab_at(first)},
+            src_ref=send.at[pl.ds(lax.rem(spot + k, GROUP) * groups, groups)],
+            dst_ref=arrived.at[k],
+            send_sem=send_sem.at[k],
+            recv_sem=recv_sem.at[k],
+            device_id={"slab": mate(k)},
             device_id_type=pl.DeviceIdType.MESH,
         )
 
-    def start_block(k, carry):
-        block_copies(k, 1).start()
-        return carry
+    def peer_copy(k):
+        return pltpu.make_async_remote_copy(
+            src_ref=group_send.at[lax.rem(group + k, groups)],
+            dst_ref=group_arrived.at[k],
+            send_sem=peer_send.at[k],
+            recv_sem=peer_recv.at[k],
+            device_id={"slab": peer(k)},
+            device_id_type=pl.DeviceIdType.MESH,
+        )
 
     def ray_copy(w):
         return pltpu.make_async_remote_copy(
@@ -165,14 +201,6 @@
             device_id_type=pl.DeviceIdType.MESH,
         )
 
-    def goes(w):
-        target = me + (w - HALF)
-        return (target >= 0) & (target < slabs)
-
-    def comes(w):
-        source = me - (w - HALF)
-        return (source >= 0) & (source < slabs)
-
     def send_rays(slots):
         for w in slots:
 
@@ -182,22 +210,18 @@
 
     for load in loads[:4]:
         load.wait()
-    spectrum = lax.dot_general(
-        dft[...], traces[...], (((1,), (1,)), ((), ())), preferred_element_type=jnp.float32
-    )
-    spectrum = spectrum[: 2 * NF] + spectrum[2 * NF :]
-    spec_high = spectrum.astype(jnp.bfloat16)
-    spec_low = (spectrum - spec_high.astype(jnp.float32)).astype(jnp.bfloat16)
-    count = spectrum.shape[1]
+    spectrum = jnp.dot(traces[...], dft[...], preferred_element_type=jnp.float32)
+    spec = (spectrum[:, : 2 * NF] + spectrum[:, 2 * NF :]).astype(jnp.bfloat16)
+    count = spec.shape[0]
     bin_row = lax.broadcasted_iota(jnp.int32, (2 * BINS, count), 0) % BINS
     bin_hot = jnp.where(bin_row == bins[...], 1.0, 0.0).T.astype(jnp.bfloat16)
     id_row = lax.broadcasted_iota(jnp.int32, (slabs, count), 0)
-    id_hot = jnp.where(id_row == ids[...], 1.0, 0.0).astype(jnp.bfloat16)
-    id_hot = jnp.concatenate([id_hot, id_hot], axis=1)
+    id_at = ids[...] % GROUP * groups + ids[...] // GROUP
+    id_hot = jnp.where(id_row == id_at, 1.0, 0.0).astype(jnp.bfloat16)
     for load in loads[4:8]:
         load.wait()
 
-    pl.semaphore_wait(barrier, slabs - 1)
+    pl.semaphore_wait(barrier, greetings)
     send_rays(OTHERS)
     for w in OTHERS:
 
@@ -206,28 +230,20 @@
             rays_here[w] = rays[w]
             beams[w] = jnp.zeros_like(beams[w])
 
-    spread_wide = pair(spread, 0)
     for chunk in range(STEPS):
-        rows = slice(2 * chunk * KLO, 2 * (chunk + 1) * KLO)
-        spec = jnp.concatenate([spec_high[rows], spec_low[rows]], axis=0)
-        spec_wide = lax.dot_general(
-            spec, spread_wide, (((0,), (0,)), ((), ())), preferred_element_type=jnp.float32
-        )
+        spec_wide = jnp.dot(spec, pair(spread, 2 * chunk), preferred_element_type=jnp.float32)
         turn_wide = jnp.dot(bin_hot, pair(slant, 2 * chunk), preferred_element_type=jnp.float32)
         spec_re, spec_im = spec_wide[:, :LANES], spec_wide[:, LANES:]
         cosine, sine = turn_wide[:, :LANES], turn_wide[:, LANES:]
         terms = jnp.concatenate(
             [spec_re * cosine + spec_im * sine, spec_im * cosine - spec_re * sine], axis=1
         )
-        high = terms.astype(jnp.bfloat16)
-        low = (terms - high.astype(jnp.float32)).astype(jnp.bfloat16)
-        partial = jnp.dot(
-            id_hot, jnp.concatenate([high, low], axis=0), preferred_element_type=jnp.float32
-        )
+        partial = jnp.dot(id_hot, terms.astype(jnp.bfloat16), preferred_element_type=jnp.float32)
         sums[:, 2 * chunk, :] = partial[:, :LANES] * scale
         sums[:, 2 * chunk + 1, :] = partial[:, LANES:] * scale
     send[...] = sums[...].astype(jnp.bfloat16)
-    lax.fori_loop(1, slabs, start_block, 0)
+    for k in range(1, GROUP):
+        mate_copy(k).start()
 
     def make_u(w, held):
         for part in range(parts):
@@ -288,11 +304,22 @@
     for load in loads[8:]:
         load.wait()
     lax.fori_loop(0, WIN, make_gauss, 0)
-    lax.fori_loop(0, 5, take_rays, 0)
-
-    arrived[0] = send[me]
-    block_copies(1, slabs - 1).wait_recv()
-    own = jnp.sum(arrived[...].astype(jnp.float32), axis=0)
+    lax.fori_loop(0, 2, take_rays, 0)
+
+    for k in range(1, GROUP):
+        mate_copy(k).wait_recv()
+    group_sum[...] = send[pl.ds(spot * groups, groups)].astype(jnp.float32) + jnp.sum(
+        arrived[1:].astype(jnp.float32), axis=0
+    )
+    group_send[...] = group_sum[...].astype(jnp.bfloat16)
+    for k in range(1, groups):
+        peer_copy(k).start()
+    lax.fori_loop(2, 4, take_rays, 0)
+
+    own = group_sum[group]
+    for k in range(1, groups):
+        peer_copy(k).wait_recv()
+        own = own + group_arrived[k].astype(jnp.float32)
     beams[HALF] = own.astype(jnp.bfloat16)
     for w in OTHERS:
 
@@ -300,14 +327,17 @@
         def _():
             beam_copy(w).start()
 
-    lax.fori_loop(5, WIN, take_rays, 0)
+    lax.fori_loop(4, WIN, take_rays, 0)
     for w in OTHERS:
 
         @pl.when(comes(w))
         def _():
             beam_copy(w).wait_recv()
 
-    block_copies(1, slabs - 1).wait_send()
+    for k in range(1, GROUP):
+        mate_copy(k).wait_send()
+    for k in range(1, groups):
+        peer_copy(k).wait_send()
     for w in OTHERS:
 
         @pl.when(goes(w))
@@ -336,6 +366,7 @@
 
 def shards(traces, centre_ids, midpoint_bins, ray_times, ray_amps, beam_lateral, footprint):
     slabs = lax.axis_size("slab")
+    groups = slabs // GROUP
     count = traces.shape[1]
     depth = ray_times.shape[4]
     columns = 2 * NF * P_SIZE
@@ -366,19 +397,24 @@
             pltpu.VMEM((count, NT), jnp.bfloat16),
             pltpu.VMEM((1, count), jnp.int32),
             pltpu.VMEM((1, count), jnp.int32),
-            pltpu.VMEM((4 * NF, NT), jnp.bfloat16),
+            pltpu.VMEM((NT, 4 * NF), jnp.bfloat16),
             pltpu.VMEM((2 * STEPS, 2 * BINS, LANES), jnp.bfloat16),
-            pltpu.VMEM((2, 4 * KLO, LANES), jnp.bfloat16),
+            pltpu.VMEM((2 * STEPS, 2 * NF, LANES), jnp.bfloat16),
             pltpu.VMEM((WIN, P_SIZE, slabs), jnp.float32),
             pltpu.VMEM((WIN, 2, slabs), jnp.int32),
             pltpu.VMEM((WIN, 2, P_SIZE, depth), jnp.float32),
             pltpu.VMEM((WIN, 2, P_SIZE, depth), jnp.float32),
             pltpu.VMEM((slabs, 2 * STEPS, LANES), jnp.float32),
             pltpu.VMEM((slabs, 2 * STEPS, LANES), jnp.bfloat16),
-            pltpu.VMEM((slabs, 2 * STEPS, LANES), jnp.bfloat16),
+            pltpu.VMEM((GROUP, groups, 2 * STEPS, LANES), jnp.bfloat16),
+            pltpu.VMEM((groups, 2 * STEPS, LANES), jnp.float32),
+            pltpu.VMEM((groups, 2 * STEPS, LANES), jnp.bfloat16),
+            pltpu.VMEM((groups, 2 * STEPS, LANES), jnp.bfloat16),
             pltpu.SemaphoreType.DMA((10,)),
-            pltpu.SemaphoreType.DMA,
-            pltpu.SemaphoreType.DMA,
+            pltpu.SemaphoreType.DMA((GROUP,)),
+            pltpu.SemaphoreType.DMA((GROUP,)),
+            pltpu.SemaphoreType.DMA((groups,)),
+            pltpu.SemaphoreType.DMA((groups,)),
             pltpu.SemaphoreType.DMA((WIN,)),
             pltpu.SemaphoreType.DMA((WIN,)),
             pltpu.SemaphoreType.DMA((WIN,)),

time: 18.8 us -> 21 us (1.12)
  Pallas kernels: 18.6 us -> 20.8 us
    pallas_call x1, Pallas kernels: 16.2 us -> 18.4 us  [shards(): pl.pallas_call(functools.partial(kernel, slabs, 1.0 / math.sqrt(NT * coun...]
where the time goes in v7:
time: 21 us; the launch traced here: 20.8 us
  Pallas kernels  20.8 us (99%)
    pallas_call x1, Pallas kernels, shards(): pl.pallas_call(functools.partial(kernel, slabs, 1.0 / math.sqrt(NT * coun...  18.4 us
    pallas_call x1, Pallas kernels, shards(): pl.pallas_call(image_kernel, out_shape=jax.ShapeDtypeStruct((depth, XW),...  2.4 us

profile of v7, /device:TPU:0, one launch (start us, length us, event | category | flops | bytes accessed | tf_op | source)
XLA Modules:
  0.0 20.8 jit_solution(14403756547075495093)
XLA Ops:
  0.0 18.4 %shard_map.100 = (bf16[7,2,2048,128]{3,2,1,0:T(8,128)(2,1)S(1)}, f32[7,128,128]{2,1,0:T(8,128)S(1)}, f32[7,128,128]{2,1,0:T(8,128)S(1)}, bf16[7,16,128]{2,1,0:T(8,128)(2,1)S(1)}) custom-call(bf16[1,128,256]{2,1,0:T(8,128)(2,1)} %traces_in.1, s32[1,128]{1,0:T(1,128)} %bitcast.5, s32[1,128]{1,0:T(1,128)} %bins_in.1, bf16[256,256]{1,0:T(8,128)(2,1)} %constant.6.clone.dft_in, ...), custom_call_target="tpu_custom_call" | custom-call | tf_op jit(solution)/shard_map/pallas_call | solution.py:386
  18.4 2.4 %shard_map.101 = f32[256,128]{1,0:T(8,128)} custom-call(bf16[7,2,2048,128]{3,2,1,0:T(8,128)(2,1)S(1)} %get-tuple-element.9.u, f32[7,128,128]{2,1,0:T(8,128)S(1)} %get-tuple-element.10.gauss, f32[7,128,128]{2,1,0:T(8,128)S(1)} %get-tuple-element.11.step, bf16[7,16,128]{2,1,0:T(8,128)(2,1)S(1)} %get-tuple-element.12.beams), custom_call_target="tpu_custom_call" | custom-call | tf_op jit(solution)/shard_map/pallas_call | solution.py:427

commit v8 on v6

--- a/solution.py
+++ b/solution.py
@@ -38,9 +38,8 @@
 
 
 def dft_halves():
-    turns = np.outer(np.arange(NF) + KLO, np.arange(NT)) % NT * (2.0 * np.pi / NT)
-    table = np.stack([np.cos(turns), -np.sin(turns)]).reshape(2, STEPS, KLO, NT)
-    return np.concatenate(halves(table.transpose(1, 0, 2, 3).reshape(2 * NF, NT)), axis=0)
+    turns = np.outer(np.arange(NT), np.arange(NF) + KLO) % NT * (2.0 * np.pi / NT)
+    return np.concatenate(halves(np.concatenate([np.cos(turns), -np.sin(turns)], axis=1)), axis=1)
 
 
 def by_chunk(table):
@@ -58,7 +57,7 @@
 
 
 def spread_table():
-    one_of = np.repeat(np.eye(2 * KLO), P_SIZE, axis=1).reshape(2 * KLO, 2, LANES).transpose(1, 0, 2)
+    one_of = by_chunk(np.repeat(np.eye(2 * NF), P_SIZE, axis=1))
     return np.concatenate([one_of, one_of], axis=1).astype(ml_dtypes.bfloat16)
 
 
@@ -182,13 +181,12 @@
 
     for load in loads[:4]:
         load.wait()
-    spectrum = lax.dot_general(
-        dft[...], traces[...], (((1,), (1,)), ((), ())), preferred_element_type=jnp.float32
-    )
-    spectrum = spectrum[: 2 * NF] + spectrum[2 * NF :]
+    spectrum = jnp.dot(traces[...], dft[...], preferred_element_type=jnp.float32)
+    spectrum = spectrum[:, : 2 * NF] + spectrum[:, 2 * NF :]
     spec_high = spectrum.astype(jnp.bfloat16)
     spec_low = (spectrum - spec_high.astype(jnp.float32)).astype(jnp.bfloat16)
-    count = spectrum.shape[1]
+    spec = jnp.concatenate([spec_high, spec_low], axis=1)
+    count = spec.shape[0]
     bin_row = lax.broadcasted_iota(jnp.int32, (2 * BINS, count), 0) % BINS
     bin_hot = jnp.where(bin_row == bins[...], 1.0, 0.0).T.astype(jnp.bfloat16)
     id_row = lax.broadcasted_iota(jnp.int32, (slabs, count), 0)
@@ -198,7 +196,7 @@
         load.wait()
 
     pl.semaphore_wait(barrier, slabs - 1)
-    send_rays(OTHERS)
+    send_rays(OTHERS[:2])
     for w in OTHERS:
 
         @pl.when(jnp.logical_not(comes(w)))
@@ -206,13 +204,8 @@
             rays_here[w] = rays[w]
             beams[w] = jnp.zeros_like(beams[w])
 
-    spread_wide = pair(spread, 0)
     for chunk in range(STEPS):
-        rows = slice(2 * chunk * KLO, 2 * (chunk + 1) * KLO)
-        spec = jnp.concatenate([spec_high[rows], spec_low[rows]], axis=0)
-        spec_wide = lax.dot_general(
-            spec, spread_wide, (((0,), (0,)), ((), ())), preferred_element_type=jnp.float32
-        )
+        spec_wide = jnp.dot(spec, pair(spread, 2 * chunk), preferred_element_type=jnp.float32)
         turn_wide = jnp.dot(bin_hot, pair(slant, 2 * chunk), preferred_element_type=jnp.float32)
         spec_re, spec_im = spec_wide[:, :LANES], spec_wide[:, LANES:]
         cosine, sine = turn_wide[:, :LANES], turn_wide[:, LANES:]
@@ -228,6 +221,7 @@
         sums[:, 2 * chunk + 1, :] = partial[:, LANES:] * scale
     send[...] = sums[...].astype(jnp.bfloat16)
     lax.fori_loop(1, slabs, start_block, 0)
+    send_rays(OTHERS[2:])
 
     def make_u(w, held):
         for part in range(parts):
@@ -288,7 +282,7 @@
     for load in loads[8:]:
         load.wait()
     lax.fori_loop(0, WIN, make_gauss, 0)
-    lax.fori_loop(0, 5, take_rays, 0)
+    lax.fori_loop(0, 3, take_rays, 0)
 
     arrived[0] = send[me]
     block_copies(1, slabs - 1).wait_recv()
@@ -300,7 +294,7 @@
         def _():
             beam_copy(w).start()
 
-    lax.fori_loop(5, WIN, take_rays, 0)
+    lax.fori_loop(3, WIN, take_rays, 0)
     for w in OTHERS:
 
         @pl.when(comes(w))
@@ -366,9 +360,9 @@
             pltpu.VMEM((count, NT), jnp.bfloat16),
             pltpu.VMEM((1, count), jnp.int32),
             pltpu.VMEM((1, count), jnp.int32),
-            pltpu.VMEM((4 * NF, NT), jnp.bfloat16),
+            pltpu.VMEM((NT, 4 * NF), jnp.bfloat16),
             pltpu.VMEM((2 * STEPS, 2 * BINS, LANES), jnp.bfloat16),
-            pltpu.VMEM((2, 4 * KLO, LANES), jnp.bfloat16),
+            pltpu.VMEM((2 * STEPS, 4 * NF, LANES), jnp.bfloat16),
             pltpu.VMEM((WIN, P_SIZE, slabs), jnp.float32),
             pltpu.VMEM((WIN, 2, slabs), jnp.int32),
             pltpu.VMEM((WIN, 2, P_SIZE, depth), jnp.float32),

time: 18.8 us -> 18.3 us (0.973)
  Pallas kernels: 18.6 us -> 18.1 us
    pallas_call x1, Pallas kernels: 16.2 us -> 15.7 us  [shards(): pl.pallas_call(functools.partial(kernel, slabs, 1.0 / math.sqrt(NT * coun...]
where the time goes in v8:
time: 18.3 us; the launch traced here: 18.2 us
  Pallas kernels  18.1 us (99%)
    pallas_call x1, Pallas kernels, shards(): pl.pallas_call(functools.partial(kernel, slabs, 1.0 / math.sqrt(NT * coun...  15.7 us
    pallas_call x1, Pallas kernels, shards(): pl.pallas_call(image_kernel, out_shape=jax.ShapeDtypeStruct((depth, XW),...  2.4 us

profile of v8, /device:TPU:0, one launch (start us, length us, event | category | flops | bytes accessed | tf_op | source)
XLA Modules:
  0.0 18.2 jit_solution(4647942076276800568)
XLA Ops:
  0.0 15.7 %shard_map.100 = (bf16[7,2,2048,128]{3,2,1,0:T(8,128)(2,1)S(1)}, f32[7,128,128]{2,1,0:T(8,128)S(1)}, f32[7,128,128]{2,1,0:T(8,128)S(1)}, bf16[7,16,128]{2,1,0:T(8,128)(2,1)S(1)}) custom-call(bf16[1,128,256]{2,1,0:T(8,128)(2,1)} %traces_in.1, s32[1,128]{1,0:T(1,128)} %bitcast.5, s32[1,128]{1,0:T(1,128)} %bins_in.1, bf16[256,256]{1,0:T(8,128)(2,1)} %constant.6.clone.dft_in, ...), custom_call_target="tpu_custom_call" | custom-call | tf_op jit(solution)/shard_map/pallas_call | solution.py:349
  15.7 2.4 %shard_map.101 = f32[256,128]{1,0:T(8,128)} custom-call(bf16[7,2,2048,128]{3,2,1,0:T(8,128)(2,1)S(1)} %get-tuple-element.9.u, f32[7,128,128]{2,1,0:T(8,128)S(1)} %get-tuple-element.10.gauss, f32[7,128,128]{2,1,0:T(8,128)S(1)} %get-tuple-element.11.step, bf16[7,16,128]{2,1,0:T(8,128)(2,1)S(1)} %get-tuple-element.12.beams), custom_call_target="tpu_custom_call" | custom-call | tf_op jit(solution)/shard_map/pallas_call | solution.py:385

commit v9 on v8

--- a/solution.py
+++ b/solution.py
@@ -57,8 +57,7 @@
 
 
 def spread_table():
-    one_of = by_chunk(np.repeat(np.eye(2 * NF), P_SIZE, axis=1))
-    return np.concatenate([one_of, one_of], axis=1).astype(ml_dtypes.bfloat16)
+    return by_chunk(np.repeat(np.eye(2 * NF), P_SIZE, axis=1)).astype(ml_dtypes.bfloat16)
 
 
 def fit_even(values, degree):
@@ -205,7 +204,12 @@
             beams[w] = jnp.zeros_like(beams[w])
 
     for chunk in range(STEPS):
-        spec_wide = jnp.dot(spec, pair(spread, 2 * chunk), preferred_element_type=jnp.float32)
+        spread_wide = pair(spread, 2 * chunk)
+        spec_wide = jnp.dot(
+            spec,
+            jnp.concatenate([spread_wide, spread_wide], axis=0),
+            preferred_element_type=jnp.float32,
+        )
         turn_wide = jnp.dot(bin_hot, pair(slant, 2 * chunk), preferred_element_type=jnp.float32)
         spec_re, spec_im = spec_wide[:, :LANES], spec_wide[:, LANES:]
         cosine, sine = turn_wide[:, :LANES], turn_wide[:, LANES:]
@@ -258,7 +262,7 @@
         held = lax.broadcasted_iota(jnp.int32, values.shape, 1) == centre
         return jnp.sum(jnp.where(held, values, 0.0), axis=1, keepdims=True)
 
-    def make_gauss(w, carry):
+    def make_gauss(w):
         axis = pick(lateral[w], w)
         axis = jnp.sum(jnp.where(slow_row == slow_lane, axis, 0.0), axis=0, keepdims=True)
         ends = pick(footprint[w].astype(jnp.float32), w)
@@ -266,7 +270,6 @@
         off = jnp.where((place >= ends[0:1]) & (place < ends[1:2]), off * off, 1e9)
         gauss[w] = jnp.exp2(off * rates) * (1.0 / math.sqrt(P_SIZE * NF))
         step[w] = jnp.exp2(off * (KLO * rate))
-        return carry
 
     def take_rays(i, carry):
         w = order(i)
@@ -281,7 +284,8 @@
     rays_here[HALF] = rays[HALF]
     for load in loads[8:]:
         load.wait()
-    lax.fori_loop(0, WIN, make_gauss, 0)
+    for w in range(WIN):
+        make_gauss(w)
     lax.fori_loop(0, 3, take_rays, 0)
 
     arrived[0] = send[me]
@@ -362,7 +366,7 @@
             pltpu.VMEM((1, count), jnp.int32),
             pltpu.VMEM((NT, 4 * NF), jnp.bfloat16),
             pltpu.VMEM((2 * STEPS, 2 * BINS, LANES), jnp.bfloat16),
-            pltpu.VMEM((2 * STEPS, 4 * NF, LANES), jnp.bfloat16),
+            pltpu.VMEM((2 * STEPS, 2 * NF, LANES), jnp.bfloat16),
             pltpu.VMEM((WIN, P_SIZE, slabs), jnp.float32),
             pltpu.VMEM((WIN, 2, slabs), jnp.int32),
             pltpu.VMEM((WIN, 2, P_SIZE, depth), jnp.float32),

time: 18.3 us -> 18.3 us (level)
  no operation moved by 1% of the time
where the time goes in v9:
time: 18.3 us; the launch traced here: 18.1 us
  Pallas kernels  18.1 us (99%)
    pallas_call x1, Pallas kernels, shards(): pl.pallas_call(functools.partial(kernel, slabs, 1.0 / math.sqrt(NT * coun...  15.7 us
    pallas_call x1, Pallas kernels, shards(): pl.pallas_call(image_kernel, out_shape=jax.ShapeDtypeStruct((depth, XW),...  2.4 us

profile of v9, /device:TPU:0, one launch (start us, length us, event | category | flops | bytes accessed | tf_op | source)
XLA Modules:
  0.0 18.1 jit_solution(12301367105901491387)
XLA Ops:
  0.0 15.7 %shard_map.100 = (bf16[7,2,2048,128]{3,2,1,0:T(8,128)(2,1)S(1)}, f32[7,128,128]{2,1,0:T(8,128)S(1)}, f32[7,128,128]{2,1,0:T(8,128)S(1)}, bf16[7,16,128]{2,1,0:T(8,128)(2,1)S(1)}) custom-call(bf16[1,128,256]{2,1,0:T(8,128)(2,1)} %traces_in.1, s32[1,128]{1,0:T(1,128)} %bitcast.5, s32[1,128]{1,0:T(1,128)} %bins_in.1, bf16[256,256]{1,0:T(8,128)(2,1)} %constant.6.clone.dft_in, ...), custom_call_target="tpu_custom_call" | custom-call | tf_op jit(solution)/shard_map/pallas_call | solution.py:353
  15.7 2.4 %shard_map.101 = f32[256,128]{1,0:T(8,128)} custom-call(bf16[7,2,2048,128]{3,2,1,0:T(8,128)(2,1)S(1)} %get-tuple-element.9.u, f32[7,128,128]{2,1,0:T(8,128)S(1)} %get-tuple-element.10.gauss, f32[7,128,128]{2,1,0:T(8,128)S(1)} %get-tuple-element.11.step, bf16[7,16,128]{2,1,0:T(8,128)(2,1)S(1)} %get-tuple-element.12.beams), custom_call_target="tpu_custom_call" | custom-call | tf_op jit(solution)/shard_map/pallas_call | solution.py:389

commit v10 on v9

--- a/solution.py
+++ b/solution.py
@@ -195,7 +195,7 @@
         load.wait()
 
     pl.semaphore_wait(barrier, slabs - 1)
-    send_rays(OTHERS[:2])
+    send_rays(OTHERS[:3])
     for w in OTHERS:
 
         @pl.when(jnp.logical_not(comes(w)))
@@ -225,7 +225,7 @@
         sums[:, 2 * chunk + 1, :] = partial[:, LANES:] * scale
     send[...] = sums[...].astype(jnp.bfloat16)
     lax.fori_loop(1, slabs, start_block, 0)
-    send_rays(OTHERS[2:])
+    send_rays(OTHERS[3:])
 
     def make_u(w, held):
         for part in range(parts):
@@ -286,7 +286,7 @@
         load.wait()
     for w in range(WIN):
         make_gauss(w)
-    lax.fori_loop(0, 3, take_rays, 0)
+    lax.fori_loop(0, 4, take_rays, 0)
 
     arrived[0] = send[me]
     block_copies(1, slabs - 1).wait_recv()
@@ -298,7 +298,7 @@
         def _():
             beam_copy(w).start()
 
-    lax.fori_loop(3, WIN, take_rays, 0)
+    lax.fori_loop(4, WIN, take_rays, 0)
     for w in OTHERS:
 
         @pl.when(comes(w))

time: 18.3 us -> 18.3 us (level)
  no operation moved by 1% of the time
where the time goes in v10:
time: 18.3 us; the launch traced here: 18.1 us
  Pallas kernels  18.1 us (99%)
    pallas_call x1, Pallas kernels, shards(): pl.pallas_call(functools.partial(kernel, slabs, 1.0 / math.sqrt(NT * coun...  15.7 us
    pallas_call x1, Pallas kernels, shards(): pl.pallas_call(image_kernel, out_shape=jax.ShapeDtypeStruct((depth, XW),...  2.4 us

profile of v10, /device:TPU:0, one launch (start us, length us, event | category | flops | bytes accessed | tf_op | source)
XLA Modules:
  0.0 18.1 jit_solution(17838550653864447116)
XLA Ops:
  0.0 15.7 %shard_map.100 = (bf16[7,2,2048,128]{3,2,1,0:T(8,128)(2,1)S(1)}, f32[7,128,128]{2,1,0:T(8,128)S(1)}, f32[7,128,128]{2,1,0:T(8,128)S(1)}, bf16[7,16,128]{2,1,0:T(8,128)(2,1)S(1)}) custom-call(bf16[1,128,256]{2,1,0:T(8,128)(2,1)} %traces_in.1, s32[1,128]{1,0:T(1,128)} %bitcast.5, s32[1,128]{1,0:T(1,128)} %bins_in.1, bf16[256,256]{1,0:T(8,128)(2,1)} %constant.6.clone.dft_in, ...), custom_call_target="tpu_custom_call" | custom-call | tf_op jit(solution)/shard_map/pallas_call | solution.py:353
  15.7 2.4 %shard_map.101 = f32[256,128]{1,0:T(8,128)} custom-call(bf16[7,2,2048,128]{3,2,1,0:T(8,128)(2,1)S(1)} %get-tuple-element.9.u, f32[7,128,128]{2,1,0:T(8,128)S(1)} %get-tuple-element.10.gauss, f32[7,128,128]{2,1,0:T(8,128)S(1)} %get-tuple-element.11.step, bf16[7,16,128]{2,1,0:T(8,128)(2,1)S(1)} %get-tuple-element.12.beams), custom_call_target="tpu_custom_call" | custom-call | tf_op jit(solution)/shard_map/pallas_call | solution.py:389
